TPU v7x, 32 devices: a whole 2x2x4 slice. The times are simulated.
32 devices in a mesh: face: 4 (over z), tile: 8 (over y, x, core).
Axes of the slice: x: 2, y: 2, z: 4, core: 2. Of those that a mesh axis runs over, the one named last changes fastest.
Arguments:
- fields: bfloat16 [768, 384, 128], P('tile', 'face'), may hold values from -6 to 6
- first_kernel_taps: bfloat16 [9, 128, 128], replicated, may hold values from -0.1875 to 0.1875
- first_conv_bias: float32 [128], replicated, may hold values from -0.5 to 0.5
- second_kernel_taps: bfloat16 [9, 128, 128], replicated, may hold values from -0.1875 to 0.1875
- second_conv_bias: float32 [128], replicated, may hold values from -0.5 to 0.5
- obs_weight: bfloat16 [128, 128], replicated, may hold values from -0.5 to 0.5
- obs_values: bfloat16 [32768, 128], P(('face', 'tile')), may hold values from -6 to 6
- obs_owner: int32 [32768, 1], P(('face', 'tile')), may hold values from 0 to 31; in each aligned block of 1024 rows (0 to 1023, 1024 to 2047, ...) at most 64 rows name the same one
- obs_cells: int32 [32768], P(('face', 'tile')), may hold values from 0 to 9215
- polar_neighbor_sector: int32 [4, 2], replicated, may hold values from 0 to 3, as said below
- polar_link_reversal: int32 [4, 2], replicated, may hold values from 0 to 1
Outputs:
- level_out: bfloat16 [768, 384, 128], P('tile', 'face')
Inputs may be any that keep to these rules, and one draw needn't show every extreme that they name: `obs_owner`: among the rows of one device at most 64 name the same tile, and in every draw some device sends exactly 64 rows to one tile. `polar_neighbor_sector`: each column links the sectors in one cycle through all 4 of them; no sector names itself.
All inputs are finite; a program needn't handle non-finite values.
Results may differ from a plain program's by a relative error of at most 0.0034.
Values may be sent and summed in bfloat16 or wider, within the bound.
A program may use at most 64 MiB of HBM per device.

v0:
```python
import math

import jax
import jax.numpy as jnp
from jax import lax
from jax.sharding import PartitionSpec as P

FIRST_DILATION = 2
SECOND_DILATION = 4


def padded_2(block, sides, width, periodic):
    for axis, dim in sides:
        count = lax.axis_size(axis)
        forward = [(i, i + 1) for i in range(count - 1)]
        if periodic:
            forward.append((count - 1, 0))
        backward = [(target, source) for source, target in forward]
        low = lax.ppermute(
            lax.slice_in_dim(block, block.shape[dim] - width, None, axis=dim), axis, forward
        )
        high = lax.ppermute(lax.slice_in_dim(block, 0, width, axis=dim), axis, backward)
        block = jnp.concatenate([low, block, high], axis=dim)
    return block


def apply_stencil_taps(padded, kernel, bias_row, dilation, rows, cols):
    channels = padded.shape[-1]
    total = jnp.zeros((rows * cols, kernel.shape[-1]), jnp.float32)
    for tap_row in range(3):
        for tap_col in range(3):
            window = padded[
                tap_row * dilation : tap_row * dilation + rows,
                tap_col * dilation : tap_col * dilation + cols,
            ]
            total = total + jnp.dot(
                window.reshape(rows * cols, channels),
                kernel[tap_row * 3 + tap_col],
                preferred_element_type=jnp.float32,
            )
    return total + bias_row[None, :]


def pad_sector_halo(tile_values, dilation, polar_neighbor_sector, polar_link_reversal):
    wide = padded_2(tile_values, (("face", 1),), dilation, True)
    tall = padded_2(wide, (("tile", 0),), dilation, False)
    sector = lax.axis_index("face")
    top_rows = wide[:dilation][::-1]
    bottom_rows = wide[wide.shape[0] - dilation :][::-1]
    want_north = polar_neighbor_sector[sector, 0]
    want_south = polar_neighbor_sector[sector, 1]
    empty_rows = jnp.zeros_like(top_rows)
    pieces = (
        lax.all_gather(top_rows, "face", axis=0, tiled=True),
        lax.all_gather(bottom_rows, "face", axis=0, tiled=True),
    )
    start = jnp.int32(0)
    north_now = empty_rows
    south_now = empty_rows
    blocks = pieces[0].shape[0] // dilation
    for offset in range(blocks):
        source = start // dilation + offset
        north_now = jnp.where(
            source == want_north, pieces[0][offset * dilation : (offset + 1) * dilation], north_now
        )
        south_now = jnp.where(
            source == want_south, pieces[1][offset * dilation : (offset + 1) * dilation], south_now
        )
    north = north_now
    south = south_now
    north = jnp.where(polar_link_reversal[sector, 0] == 1, north[:, ::-1], north)
    south = jnp.where(polar_link_reversal[sector, 1] == 1, south[:, ::-1], south)
    lat_place = lax.axis_index("tile")
    last_place = lax.axis_size("tile") - 1
    total_rows = tall.shape[0]
    upper = jnp.where(lat_place == 0, north, tall[:dilation])
    lower = jnp.where(lat_place == last_place, south, tall[total_rows - dilation :])
    return jnp.concatenate([upper, tall[dilation : total_rows - dilation], lower], axis=0)


def owner_ranks(owner, dest_count):
    obs_rows = owner.shape[0]
    block_rows = math.gcd(obs_rows, 512)
    block_count = obs_rows // block_rows
    onehot = (owner[:, None] == jnp.arange(dest_count, dtype=jnp.int32)[None, :]).astype(
        jnp.bfloat16
    )
    blocked = onehot.reshape(block_count, block_rows, dest_count)
    lower = (
        jnp.arange(block_rows, dtype=jnp.int32)[:, None]
        > jnp.arange(block_rows, dtype=jnp.int32)[None, :]
    ).astype(jnp.bfloat16)

    def one_block(carry, block):
        inside = jnp.dot(lower, block, preferred_element_type=jnp.float32) + carry[None, :]
        return (carry + jnp.sum(block.astype(jnp.float32), axis=0), inside)

    init_carry = jnp.zeros((dest_count,), jnp.float32)
    unused, ranks = lax.scan(one_block, init_carry, blocked)
    ranks = ranks.reshape(obs_rows, dest_count)
    return jnp.sum(ranks * onehot.astype(jnp.float32), axis=1).astype(jnp.int32)


def local(
    fields,
    first_kernel_taps,
    first_conv_bias,
    second_kernel_taps,
    second_conv_bias,
    obs_weight,
    obs_values,
    obs_owner,
    obs_cells,
    polar_neighbor_sector,
    polar_link_reversal,
):
    sector_side_length = fields.shape[0]
    channels = fields.shape[2]
    feature_count = obs_values.shape[1]
    face_count = lax.axis_size("face")
    tile_count = lax.axis_size("tile")
    dest_count = face_count * tile_count
    obs_rows = obs_values.shape[0]
    slots = 2 * obs_rows // dest_count
    cell_total = sector_side_length * sector_side_length
    owner = obs_owner[:, 0]
    slot_index = owner_ranks(owner, dest_count)
    target = owner * slots + slot_index
    slot_total = dest_count * slots
    slot_block = math.gcd(slot_total, 512)

    def fill_slots(base):
        wanted = base + jnp.arange(slot_block, dtype=jnp.int32)
        match = target[None, :] == wanted[:, None]
        rows = jnp.dot(
            match.astype(jnp.bfloat16), obs_values, preferred_element_type=jnp.float32
        ).astype(jnp.bfloat16)
        hit = jnp.any(match, axis=1)
        cell_sum = jnp.sum(jnp.where(match, obs_cells[None, :], 0), axis=1)
        return (rows, jnp.where(hit, cell_sum, cell_total))

    slot_bases = jnp.arange(slot_total // slot_block, dtype=jnp.int32) * slot_block
    send_rows, send_cells = lax.map(fill_slots, slot_bases)
    send_rows = send_rows.reshape(slot_total, feature_count)
    send_cells = send_cells.reshape(slot_total)
    direct_rows = send_rows.reshape(dest_count, slots, feature_count)
    direct_cells = send_cells.reshape(dest_count, slots)
    recv_rows, recv_cells = (
        lax.all_to_all(direct_rows, ("face", "tile"), split_axis=0, concat_axis=0, tiled=True),
        lax.all_to_all(direct_cells, ("face", "tile"), split_axis=0, concat_axis=0, tiled=True),
    )
    first_padded_grid = pad_sector_halo(
        fields, FIRST_DILATION, polar_neighbor_sector, polar_link_reversal
    )
    first_activation = jax.nn.gelu(
        apply_stencil_taps(
            first_padded_grid,
            first_kernel_taps,
            first_conv_bias,
            FIRST_DILATION,
            sector_side_length,
            sector_side_length,
        ),
        approximate=True,
    )
    flat_rows = recv_rows.reshape(-1, feature_count)
    flat_cells = recv_cells.reshape(-1)
    cell_block = math.gcd(cell_total, 2048)

    def gather_cells(base):
        wanted = base + jnp.arange(cell_block, dtype=jnp.int32)
        match = (flat_cells[None, :] == wanted[:, None]).astype(jnp.bfloat16)
        return jnp.dot(match, flat_rows, preferred_element_type=jnp.float32)

    cell_bases = jnp.arange(cell_total // cell_block, dtype=jnp.int32) * cell_block
    summed_rows = lax.map(gather_cells, cell_bases).reshape(cell_total, feature_count)
    inject = jnp.dot(
        summed_rows,
        obs_weight.astype(jnp.float32),
        precision=lax.Precision.HIGHEST,
        preferred_element_type=jnp.float32,
    )
    blended_features = (
        (first_activation + inject)
        .astype(jnp.bfloat16)
        .reshape(sector_side_length, sector_side_length, channels)
    )
    second_padded_grid = pad_sector_halo(
        blended_features, SECOND_DILATION, polar_neighbor_sector, polar_link_reversal
    )
    second_activation = apply_stencil_taps(
        second_padded_grid,
        second_kernel_taps,
        second_conv_bias,
        SECOND_DILATION,
        sector_side_length,
        sector_side_length,
    )
    level_out = fields.astype(jnp.float32).reshape(cell_total, channels) + jax.nn.gelu(
        second_activation, approximate=True
    )
    return level_out.astype(jnp.bfloat16).reshape(sector_side_length, sector_side_length, channels)


def solution(mesh):
    in_specs = (
        P("tile", "face", None),
        P(),
        P(),
        P(),
        P(),
        P(),
        P(("face", "tile"), None),
        P(("face", "tile"), None),
        P(("face", "tile")),
        P(),
        P(),
    )
    out_specs = P("tile", "face", None)
    return jax.shard_map(local, mesh=mesh, in_specs=in_specs, out_specs=out_specs, check_vma=False)
```

profile of v0, /device:TPU:0, one launch (start us, length us, event | category | flops | bytes accessed | tf_op | source)
XLA Modules:
  0.0 222.6 jit_solution(13821982820846365413)
XLA Ops:
  1.3 3.1 %collective-permute-start = (bf16[96,2,128]{2,1,0:T(2,128)(2,1)S(1)}, bf16[96,2,128]{2,1,0:T(2,128)(2,1)S(1)}, u32[]{:S(2)}, u32[]{:S(2)}) collective-permute-start(bf16[96,2,128]{2,1,0:T(2,128)(2,1)S(1)} %get-tuple-element.190), channel_id=1, source_target_pairs={{0,8},{8,16},{16,24},{24,0},{1,9},{9,17},{17,25},{25,1},{2,10},{10... | collective-permute-start | bytes 147464 | tf_op jit(solution)/shard_map/ppermute | solution.py:19
  9.3 19.3 %while.36 = (s32[]{:T(128)}, bf16[4,512,128]{2,1,0:T(8,128)(2,1)}, s32[4,512]{1,0:T(4,128)S(1)}, s32[1024]{0:T(1024)S(1)}, s32[4]{0:T(128)S(1)}, /*index=5*/bf16...) while((s32[]{:T(128)}, bf16[4,512,128]{2,1,0:T(8,128)(2,1)}, s32[4,512]{1,0:T(4,128)S(1)}, ...), condition=%wide.region_7.8_spmd, body=%wide.region_4.7_spmd.sunk | while | flops 137428992 | bytes 429681 | solution.py:143
  29.3 4.2 %all-to-all-start = ((s32[32,1,64]{2,1,0:T(1,128)}), s32[32,1,64]{2,1,0:T(1,128)S(1)}, u32[]{:S(2)}, u32[]{:S(2)}) async-start(s32[32,1,64]{2,1,0:T(1,128)} %all_to_all.11), calls=%async_computation | async-start | bytes 32768 | tf_op jit(solution)/shard_map/all_to_all | solution.py:150
  33.6 3.7 %fusion.84 = f32[9216,128]{1,0:T(8,128)} fusion(bf16[9216,128]{1,0:T(8,128)(2,1)S(1)} %bitcast.163, bf16[9,128,128]{2,1,0:T(8,128)(2,1)} %param.18), kind=kOutput, calls=%fused_computation.121 | convolution fusion | flops 301989888 | bytes 7110656 | tf_op jit(solution)/shard_map/dot_general | solution.py:36
  44.9 5.8 %all-to-all-start.1 = ((bf16[32,64,128]{2,1,0:T(8,128)(2,1)}), bf16[32,64,128]{2,1,0:T(8,128)(2,1)S(1)}, u32[]{:S(2)}, u32[]{:S(2)}) async-start(bf16[32,64,128]{2,1,0:T(8,128)(2,1)} %bitcast.35), calls=%async_computation.1 | async-start | bytes 1048576 | tf_op jit(solution)/shard_map/all_to_all | solution.py:149
  54.5 3.6 %collective-permute-start.2 = (bf16[2,100,128]{2,1,0:T(8,128)(2,1)}, bf16[2,100,128]{2,1,0:T(8,128)(2,1)}, u32[]{:S(2)}, u32[]{:S(2)}) collective-permute-start(bf16[2,100,128]{2,1,0:T(8,128)(2,1)} %get-tuple-element.182), channel_id=1, source_target_pairs={{0,1},{1,2},{2,3},{3,4},{4,5},{5,6},{6,7},{8,9},{9,10},{10,11},{11... | collective-permute-start | bytes 153608 | tf_op jit(solution)/shard_map/ppermute | solution.py:19
  58.1 14.3 %all_gather.13 = bf16[8,100,128]{2,1,0:T(8,128)(2,1)S(1)} all-gather(bf16[2,100,128]{2,1,0:T(8,128)(2,1)S(1)} %rev.26), channel_id=1, replica_groups=mesh['face'=4,'tile'=8] {'face'}, dimensions={0}, use_global_device_ids=true | all-gather | bytes 256000 | tf_op jit(solution)/shard_map/all_gather | solution.py:55
  72.4 13.7 %all_gather.12 = bf16[8,100,128]{2,1,0:T(8,128)(2,1)S(1)} all-gather(bf16[2,100,128]{2,1,0:T(8,128)(2,1)S(1)} %rev.24), channel_id=1, replica_groups=mesh['face'=4,'tile'=8] {'face'}, dimensions={0}, use_global_device_ids=true | all-gather | bytes 256000 | tf_op jit(solution)/shard_map/all_gather | solution.py:54
  86.2 3.6 %pad_maximum_fusion.4 = (bf16[96,96,128]{2,1,0:T(8,128)(2,1)}, bf16[96,96,128]{2,1,0:T(8,128)(2,1)}) fusion(bf16[96,2,128]{2,1,0:T(2,128)(2,1)S(1)} %collective-permute-done.1, bf16[96,96,128]{2,1,0:T(8,128)(2,1)S(1)} %copy-done.2, bf16[96,2,128]{2,1,0:T(2,128)(2,1)S(1)} %collective-permute-done), kind=kLoop, calls=%fused_computation.73 | loop fusion | flops 9437184 | bytes 7176192 | tf_op jit(solution)/shard_map/concatenate | solution.py:23
  92.3 4.3 %maximum_maximum_fusion.1 = (bf16[98,100,128]{2,1,0:T(8,128)(2,1)S(1)}, bf16[98,100,128]{2,1,0:T(8,128)(2,1)S(1)}) fusion(bf16[96,2,128]{2,1,0:T(2,128)(2,1)S(1)} %collective-permute-done.1, bf16[96,96,128]{2,1,0:T(8,128)(2,1)S(1)} %copy-done.2, bf16[96,2,128]{2,1,0:T(2,128)(2,1)S(1)} %collective-permute-done, ...), kind=kLoop, calls=%fused_computation.69 | loop fusion | flops 20070400 | bytes 7577600 | tf_op jit(solution)/shard_map/concatenate | solution.py:78
  107.3 4.0 %fusion.44 = f32[9216,128]{1,0:T(8,128)} fusion(f32[9216,128]{1,0:T(8,128)S(1)} %convolution_add_fusion.9, bf16[9216,128]{1,0:T(8,128)(2,1)S(1)} %bitcast.184, f32[128]{0:T(128)S(1)} %copy-done.14, bf16[9,128,128]{2,1,0:T(8,128)(2,1)S(1)} %copy-done.9), kind=kOutput, calls=%fused_computation.57 | convolution fusion | flops 313786368 | bytes 11829760 | tf_op jit(solution)/shard_map/dot_general | solution.py:36
  111.3 30.3 %while.38 = (s32[]{:T(128)}, f32[9,1024,128]{2,1,0:T(8,128)}, s32[32,64]{1,0:T(8,128)}, s32[9]{0:T(128)S(1)}, bf16[2048,128]{1,0:T(8,128)(2,1)S(1)}, /*index=5*/s32[2048]{0:T(1024)S(1)}, s32[]{:T(128)}) while((s32[]{:T(128)}, f32[9,1024,128]{2,1,0:T(8,128)}, s32[32,64]{1,0:T(8,128)}, s32[9]{0:T(128)S(1)}, ...), condition=%wide.wide.region_9.10_spmd, body=%wide.wide.region_8.9_spmd.sunk | while | flops 538969088 | bytes 1065565 | solution.py:176
  129.3 2.2 fusion.163
  132.7 2.1 fusion.163
  136.1 2.2 fusion.163
  141.6 6.1 %fusion.37 = bf16[9216,128]{1,0:T(8,128)(2,1)S(1)} fusion(f32[9216,128]{1,0:T(8,128)} %fusion.44, f32[9216,128]{1,0:T(8,128)} %bitcast.183, bf16[128,128]{1,0:T(8,128)(2,1)S(1)} %copy-done), kind=kOutput, calls=%fused_computation.48 | convolution fusion | flops 1814298624 | bytes 11829248 | tf_op jit(solution)/shard_map/dot_general | solution.py:177
  149.5 2.2 collective-permute-start.5
  151.6 3.7 %fusion.72 = f32[9216,128]{1,0:T(8,128)} fusion(bf16[9216,128]{1,0:T(8,128)(2,1)S(1)} %fusion.37, bf16[9,128,128]{2,1,0:T(8,128)(2,1)} %param.20), kind=kOutput, calls=%fused_computation.109 | convolution fusion | flops 301989888 | bytes 7110656 | tf_op jit(solution)/shard_map/dot_general | solution.py:36
  159.1 3.7 %collective-permute-start.6 = (bf16[4,104,128]{2,1,0:T(8,128)(2,1)}, bf16[4,104,128]{2,1,0:T(8,128)(2,1)}, u32[]{:S(2)}, u32[]{:S(2)}) collective-permute-start(bf16[4,104,128]{2,1,0:T(8,128)(2,1)} %get-tuple-element.178), channel_id=1, source_target_pairs={{0,1},{1,2},{2,3},{3,4},{4,5},{5,6},{6,7},{8,9},{9,10},{10,11},{11... | collective-permute-start | bytes 319496 | tf_op jit(solution)/shard_map/ppermute | solution.py:19
  162.8 15.3 %all_gather.15 = bf16[16,104,128]{2,1,0:T(8,128)(2,1)S(1)} all-gather(bf16[4,104,128]{2,1,0:T(8,128)(2,1)S(1)} %rev.30), channel_id=1, replica_groups=mesh['face'=4,'tile'=8] {'face'}, dimensions={0}, use_global_device_ids=true | all-gather | bytes 532480 | tf_op jit(solution)/shard_map/all_gather | solution.py:55
  178.8 14.6 %all_gather.14 = bf16[16,104,128]{2,1,0:T(8,128)(2,1)S(1)} all-gather(bf16[4,104,128]{2,1,0:T(8,128)(2,1)S(1)} %rev.28), channel_id=1, replica_groups=mesh['face'=4,'tile'=8] {'face'}, dimensions={0}, use_global_device_ids=true | all-gather | bytes 532480 | tf_op jit(solution)/shard_map/all_gather | solution.py:54
  193.3 3.6 %pad_maximum_fusion.2 = (bf16[96,96,128]{2,1,0:T(8,128)(2,1)}, bf16[96,96,128]{2,1,0:T(8,128)(2,1)}) fusion(bf16[96,4,128]{2,1,0:T(4,128)(2,1)S(1)} %collective-permute-done.5, bf16[96,96,128]{2,1,0:T(8,128)(2,1)S(1)} %bitcast.161, bf16[96,4,128]{2,1,0:T(4,128)(2,1)S(1)} %collective-permute-done.4), kind=kLoop, calls=%fused_computation.71 | loop fusion | flops 9437184 | bytes 7274496 | tf_op jit(solution)/shard_map/concatenate | solution.py:23
  201.5 4.7 %maximum_maximum_fusion = (bf16[100,104,128]{2,1,0:T(8,128)(2,1)S(1)}, bf16[100,104,128]{2,1,0:T(8,128)(2,1)S(1)}) fusion(bf16[96,4,128]{2,1,0:T(4,128)(2,1)S(1)} %collective-permute-done.5, bf16[96,96,128]{2,1,0:T(8,128)(2,1)S(1)} %bitcast.162, bf16[96,4,128]{2,1,0:T(4,128)(2,1)S(1)} %collective-permute-done.4, ...), kind=kLoop, calls=%fused_computation.67 | loop fusion | flops 21299200 | bytes 8093696 | tf_op jit(solution)/shard_map/concatenate | solution.py:78
  219.1 3.5 %fusion.53 = bf16[9216,128]{1,0:T(8,128)(2,1)} fusion(f32[9216,128]{1,0:T(8,128)S(1)} %convolution_add_fusion.2, bf16[9216,128]{1,0:T(8,128)(2,1)S(1)} %bitcast.185, bf16[9216,128]{1,0:T(8,128)(2,1)S(1)} %bitcast.164, f32[128]{0:T(128)S(1)} %copy-done.15, bf16[9,128,128]{2,1,0:T(8,128)(2,1)S(1)} %copy-done.10), kind=kOutput, calls=%fused_computation.66 | convolution fusion | flops 317325312 | bytes 11829760 | tf_op jit(solution)/shard_map/dot_general | solution.py:36
  (177 shorter events, 92.5 us)
Async XLA Ops:
  0.0 141.6 %copy-start = (bf16[128,128]{1,0:T(8,128)(2,1)S(1)}, bf16[128,128]{1,0:T(8,128)(2,1)}, u32[]{:S(2)}) copy-start(bf16[128,128]{1,0:T(8,128)(2,1)} %param.22) | copy-start | bytes 98308
  0.0 33.5 %copy-start.2 = (bf16[96,96,128]{2,1,0:T(8,128)(2,1)S(1)}, bf16[96,96,128]{2,1,0:T(8,128)(2,1)}, u32[]{:S(2)}) copy-start(bf16[96,96,128]{2,1,0:T(8,128)(2,1)} %param.17) | copy-start | bytes 7077892
  1.3 49.6 %collective-permute-start = (bf16[96,2,128]{2,1,0:T(2,128)(2,1)S(1)}, bf16[96,2,128]{2,1,0:T(2,128)(2,1)S(1)}, u32[]{:S(2)}, u32[]{:S(2)}) collective-permute-start(bf16[96,2,128]{2,1,0:T(2,128)(2,1)S(1)} %get-tuple-element.190), channel_id=1, source_target_pairs={{0,8},{8,16},{16,24},{24,0},{1,9},{9,17},{17,25},{25,1},{2,10},{10... | collective-permute-start | bytes 147464 | tf_op jit(solution)/shard_map/ppermute | solution.py:19
  4.3 46.5 %collective-permute-start.1 = (bf16[96,2,128]{2,1,0:T(2,128)(2,1)S(1)}, bf16[96,2,128]{2,1,0:T(2,128)(2,1)S(1)}, u32[]{:S(2)}, u32[]{:S(2)}) collective-permute-start(bf16[96,2,128]{2,1,0:T(2,128)(2,1)S(1)} %get-tuple-element.191), channel_id=1, source_target_pairs={{8,0},{16,8},{24,16},{0,24},{9,1},{17,9},{25,17},{1,25},{10,2},{18... | collective-permute-start | bytes 147464 | tf_op jit(solution)/shard_map/ppermute | solution.py:22
  29.3 15.6 %all-to-all-start = ((s32[32,1,64]{2,1,0:T(1,128)}), s32[32,1,64]{2,1,0:T(1,128)S(1)}, u32[]{:S(2)}, u32[]{:S(2)}) async-start(s32[32,1,64]{2,1,0:T(1,128)} %all_to_all.11), calls=%async_computation | async-start | bytes 32768 | tf_op jit(solution)/shard_map/all_to_all | solution.py:150
  33.5 4.2 %copy-start.12 = (s32[4,2]{0,1:T(2,128)S(1)}, s32[4,2]{0,1:T(2,128)}, u32[]{:S(2)}) copy-start(s32[4,2]{0,1:T(2,128)} %param.26) | copy-start | bytes 100
  33.6 4.2 %copy-start.13 = (s32[4,2]{0,1:T(2,128)S(1)}, s32[4,2]{0,1:T(2,128)}, u32[]{:S(2)}) copy-start(s32[4,2]{0,1:T(2,128)} %param.27) | copy-start | bytes 100
  44.9 8.7 %copy-start.11 = (s32[32,1,64]{2,1,0:T(1,128)}, s32[32,1,64]{2,1,0:T(1,128)S(1)}, u32[]{:S(2)}) copy-start(s32[32,1,64]{2,1,0:T(1,128)S(1)} %all-to-all-done) | copy-start | bytes 24580
  44.9 66.4 %all-to-all-start.1 = ((bf16[32,64,128]{2,1,0:T(8,128)(2,1)}), bf16[32,64,128]{2,1,0:T(8,128)(2,1)S(1)}, u32[]{:S(2)}, u32[]{:S(2)}) async-start(bf16[32,64,128]{2,1,0:T(8,128)(2,1)} %bitcast.35), calls=%async_computation.1 | async-start | bytes 1048576 | tf_op jit(solution)/shard_map/all_to_all | solution.py:149
  51.5 39.8 %collective-permute-start.3 = (bf16[2,100,128]{2,1,0:T(8,128)(2,1)}, bf16[2,100,128]{2,1,0:T(8,128)(2,1)}, u32[]{:S(2)}, u32[]{:S(2)}) collective-permute-start(bf16[2,100,128]{2,1,0:T(8,128)(2,1)} %get-tuple-element.183), channel_id=1, source_target_pairs={{1,0},{2,1},{3,2},{4,3},{5,4},{6,5},{7,6},{9,8},{10,9},{11,10},{12... | collective-permute-start | bytes 153608 | tf_op jit(solution)/shard_map/ppermute | solution.py:22
  54.5 37.7 %collective-permute-start.2 = (bf16[2,100,128]{2,1,0:T(8,128)(2,1)}, bf16[2,100,128]{2,1,0:T(8,128)(2,1)}, u32[]{:S(2)}, u32[]{:S(2)}) collective-permute-start(bf16[2,100,128]{2,1,0:T(8,128)(2,1)} %get-tuple-element.182), channel_id=1, source_target_pairs={{0,1},{1,2},{2,3},{3,4},{4,5},{5,6},{6,7},{8,9},{9,10},{10,11},{11... | collective-permute-start | bytes 153608 | tf_op jit(solution)/shard_map/ppermute | solution.py:19
  100.9 2.9 %slice-start = ((s8[4718592]{0:T(1024)(128)(4,1)}), s8[4194304]{0:T(1024)(128)(4,1)S(1)}, s32[]{:S(2)}) async-start(s8[4718592]{0:T(1024)(128)(4,1)} %bitcast.165), calls=%async_computation.2 | async-start | bytes 8388608
  101.6 2.4 %slice-start.1 = ((s8[4718592]{0:T(1024)(128)(4,1)}), s8[524288]{0:T(1024)(128)(4,1)S(1)}, s32[]{:S(2)}) async-start(s8[4718592]{0:T(1024)(128)(4,1)} %bitcast.165), calls=%async_computation.3 | async-start | bytes 1048576
  101.7 2.4 %copy-start.7 = (bf16[96,96,128]{2,1,0:T(8,128)(2,1)S(1)}, bf16[96,96,128]{2,1,0:T(8,128)(2,1)}, u32[]{:S(2)}) copy-start(bf16[96,96,128]{2,1,0:T(8,128)(2,1)} %get-tuple-element.189) | copy-start | bytes 7077892
  107.3 4.0 %copy-start.16 = (s32[9]{0:T(128)S(1)}, s32[9]{0:T(128)}, u32[]{:S(2)}) copy-start(s32[9]{0:T(128)} %iota_multiply_fusion) | copy-start | bytes 112
  147.8 7.5 %collective-permute-start.4 = (bf16[96,4,128]{2,1,0:T(4,128)(2,1)S(1)}, bf16[96,4,128]{2,1,0:T(4,128)(2,1)S(1)}, u32[]{:S(2)}, u32[]{:S(2)}) collective-permute-start(bf16[96,4,128]{2,1,0:T(4,128)(2,1)S(1)} %get-tuple-element.186), channel_id=1, source_target_pairs={{0,8},{8,16},{16,24},{24,0},{1,9},{9,17},{17,25},{25,1},{2,10},{10... | collective-permute-start | bytes 294920 | tf_op jit(solution)/shard_map/ppermute | solution.py:19
  149.5 5.8 %collective-permute-start.5 = (bf16[96,4,128]{2,1,0:T(4,128)(2,1)S(1)}, bf16[96,4,128]{2,1,0:T(4,128)(2,1)S(1)}, u32[]{:S(2)}, u32[]{:S(2)}) collective-permute-start(bf16[96,4,128]{2,1,0:T(4,128)(2,1)S(1)} %get-tuple-element.187), channel_id=1, source_target_pairs={{8,0},{16,8},{24,16},{0,24},{9,1},{17,9},{25,17},{1,25},{10,2},{18... | collective-permute-start | bytes 294920 | tf_op jit(solution)/shard_map/ppermute | solution.py:22
  156.1 44.4 %collective-permute-start.7 = (bf16[4,104,128]{2,1,0:T(8,128)(2,1)}, bf16[4,104,128]{2,1,0:T(8,128)(2,1)}, u32[]{:S(2)}, u32[]{:S(2)}) collective-permute-start(bf16[4,104,128]{2,1,0:T(8,128)(2,1)} %get-tuple-element.179), channel_id=1, source_target_pairs={{1,0},{2,1},{3,2},{4,3},{5,4},{6,5},{7,6},{9,8},{10,9},{11,10},{12... | collective-permute-start | bytes 319496 | tf_op jit(solution)/shard_map/ppermute | solution.py:22
  159.1 42.2 %collective-permute-start.6 = (bf16[4,104,128]{2,1,0:T(8,128)(2,1)}, bf16[4,104,128]{2,1,0:T(8,128)(2,1)}, u32[]{:S(2)}, u32[]{:S(2)}) collective-permute-start(bf16[4,104,128]{2,1,0:T(8,128)(2,1)} %get-tuple-element.178), channel_id=1, source_target_pairs={{0,1},{1,2},{2,3},{3,4},{4,5},{5,6},{6,7},{8,9},{9,10},{10,11},{11... | collective-permute-start | bytes 319496 | tf_op jit(solution)/shard_map/ppermute | solution.py:19
  193.3 4.2 %copy-start.8 = (bf16[4,104,128]{2,1,0:T(8,128)(2,1)S(1)}, bf16[4,104,128]{2,1,0:T(8,128)(2,1)}, u32[]{:S(2)}) copy-start(bf16[4,104,128]{2,1,0:T(8,128)(2,1)} %fusion.57) | copy-start | bytes 319492
  206.2 1.9 copy-start.10
  211.5 2.2 slice-start.2
  212.3 2.5 %copy-start.5 = (bf16[96,96,128]{2,1,0:T(8,128)(2,1)S(1)}, bf16[96,96,128]{2,1,0:T(8,128)(2,1)}, u32[]{:S(2)}) copy-start(bf16[96,96,128]{2,1,0:T(8,128)(2,1)} %get-tuple-element.185) | copy-start | bytes 7077892
  218.3 4.4 %copy-start.1 = (bf16[128,128]{1,0:T(8,128)(2,1)S(1)}, bf16[128,128]{1,0:T(8,128)(2,1)}, u32[]{:S(2)}) copy-start(bf16[128,128]{1,0:T(8,128)(2,1)} %param.22) | copy-start | bytes 98308
  (7 other events, 10.6 us)
where the time goes:
time: 225 us; the launch traced here: 223 us
  matrix products  60 us (27%)
  blocking collectives  57.9 us (26%)
  other arithmetic  37.4 us (17%)
  local copies, waits for them, and re-layouts  31.1 us (14%)
  starting transfers between devices  29 us (13%)
  between operations  6.99 us (3%)
    all_gather x2, blocking collectives, pad_sector_halo(): lax.all_gather(bottom_rows, 'face', axis=0, tiled=True)  29.6 us
    all_gather x2, blocking collectives, pad_sector_halo(): lax.all_gather(top_rows, 'face', axis=0, tiled=True)  28.3 us
    dot_general x18, matrix products, apply_stencil_taps(): jnp.dot(window.reshape(rows * cols, channels), kernel[tap_row * 3 + tap_c...  25.9 us
    dot_general x9, matrix products, gather_cells(): return jnp.dot(match, flat_rows, preferred_element_type=jnp.float32)  19.2 us
    ppermute x4, starting transfers between devices, padded_2(): lax.ppermute(lax.slice_in_dim(block, block.shape[dim] - width, None, axis...  12.1 us
    concatenate x2, other arithmetic, pad_sector_halo(): jnp.concatenate([upper, tall[dilation:total_rows - dilation], lower], axi...  8.96 us
    concatenate x4, other arithmetic, padded_2(): block = jnp.concatenate([low, block, high], axis=dim)  8.58 us
    dot_general x4, matrix products, fill_slots(): jnp.dot(match.astype(jnp.bfloat16), obs_values, preferred_element_type=jn...  8.43 us
  transfers between devices with their start and end apart: 10, of which 0 were waited for; matrix products, arithmetic and copies ran while one was open for 30% of the time, Pallas kernels for 0%

commit v1 on v0

v1 whole, which is shorter than its diff:
```python
import functools

import jax
import jax.numpy as jnp
from jax import lax
from jax.experimental import pallas as pl
from jax.experimental.pallas import tpu as pltpu
from jax.sharding import PartitionSpec as P

FIRST_DILATION = 2
SECOND_DILATION = 4
MESH = pl.DeviceIdType.MESH
LANES = 128
EDGE = 16
VMEM_LIMIT = 56 * 1024 * 1024


def pack_columns(tile, d, east):
    rows, _, ch = tile.shape
    per = 8 // d
    half = tile[:, 8:] if east else tile[:, :8]
    grouped = half.reshape(rows // per, per, 8, ch)
    sub = lax.broadcasted_iota(jnp.int32, (rows // per, 8, ch), 1)
    out = None
    for j in range(per):
        shift = (j * d - (8 - d if east else 0)) % 8
        part = grouped[:, j]
        if shift:
            part = pltpu.roll(part, shift, 1)
        out = part if out is None else jnp.where(sub >= j * d, part, out)
    return out.reshape(rows // (2 * per), EDGE, ch).astype(jnp.bfloat16)


def unpack_columns(packed, d, west):
    count, _, ch = packed.shape
    per = 8 // d
    pieces = packed.astype(jnp.float32).reshape(2 * count, 8, ch)
    parts = []
    for j in range(per):
        shift = ((8 - d if west else 0) - j * d) % 8
        parts.append(pltpu.roll(pieces, shift, 1) if shift else pieces)
    return jnp.stack(parts, axis=1).reshape(2 * count * per, 8, ch)


def join_edge(east_tile, west_tile):
    east = east_tile.astype(jnp.float32)
    west = west_tile.astype(jnp.float32)
    axis = east.ndim - 2
    return jnp.concatenate(
        [lax.slice_in_dim(east, 0, 8, axis=axis), lax.slice_in_dim(west, 8, 16, axis=axis)], axis=axis
    ).astype(jnp.bfloat16)


def pack_kernel(
    dest_count, slots, cell_total, d,
    owner_ref, cells_ref, values_ref, west_ref, east_ref,
    rows_out, cells_out, pw_out, pe_out,
):
    obs = owner_ref.shape[1]
    owner = owner_ref[...]
    dests = lax.broadcasted_iota(jnp.int32, (dest_count, obs), 0)
    onehot = jnp.where(dests == owner, 1.0, 0.0)
    before = (
        lax.broadcasted_iota(jnp.int32, (obs, obs), 0) < lax.broadcasted_iota(jnp.int32, (obs, obs), 1)
    )
    ranks = jnp.dot(
        onehot.astype(jnp.bfloat16),
        jnp.where(before, 1.0, 0.0).astype(jnp.bfloat16),
        preferred_element_type=jnp.float32,
    )
    rank = jnp.sum(ranks * onehot, axis=0, keepdims=True).astype(jnp.int32)
    target = owner * slots + rank
    cells = cells_ref[...]
    kind = lax.broadcasted_iota(jnp.int32, (8, obs), 0)
    codes = jnp.where(kind == 0, cells // LANES, jnp.where(kind == 1, cells % LANES, 1))
    codes = codes.astype(jnp.float32).astype(jnp.bfloat16)
    cells_out[...] = jnp.full(cells_out.shape, cell_total, jnp.int32)
    values = values_ref[...]
    block = min(512, dest_count * slots)
    for base in range(0, dest_count * slots, block):
        wanted = base + lax.broadcasted_iota(jnp.int32, (block, obs), 0)
        match = jnp.where(wanted == target, 1.0, 0.0).astype(jnp.bfloat16)
        rows = jnp.dot(match, values, preferred_element_type=jnp.float32).astype(jnp.bfloat16)
        first = base // slots
        rows_out[first : first + block // slots] = rows.reshape(block // slots, slots, rows.shape[-1])
        got = lax.dot_general(
            codes, match, (((1,), (1,)), ((), ())), preferred_element_type=jnp.float32
        )
        found = (got[0:1] * LANES + got[1:2]).astype(jnp.int32)
        found = jnp.where(got[2:3] > 0.5, found, cell_total)
        for j in range(block // slots):
            cells_out[first + j, :, :slots] = found[:, j * slots : (j + 1) * slots]
    pw_out[...] = pack_columns(west_ref[...].astype(jnp.float32), d, False)
    pe_out[...] = pack_columns(east_ref[...].astype(jnp.float32), d, True)


def halo_sends(faces, tiles, d, grid, pw, pe, hw, he, north, south, corners, polar):
    s, t = lax.axis_index("face"), lax.axis_index("tile")
    rows, cols = grid.shape[0], grid.shape[1]
    east, west = lax.rem(s + 1, faces), lax.rem(s + faces - 1, faces)
    last, first = pl.ds(rows - d, d), pl.ds(0, d)
    right, left = pl.ds(cols - EDGE, EDGE), pl.ds(0, EDGE)
    not_top, not_low = t > 0, t < tiles - 1
    up, down = t - 1, t + 1
    plan = [
        (None, None, pe, hw, (east, t)),
        (None, None, pw, he, (west, t)),
        (not_low, not_top, grid.at[last], north, (s, down)),
        (not_top, not_low, grid.at[first], south, (s, up)),
        (not_low, not_top, grid.at[last, right], corners.at[0], (east, down)),
        (not_low, not_top, grid.at[last, left], corners.at[1], (west, down)),
        (not_top, not_low, grid.at[first, right], corners.at[2], (east, up)),
        (not_top, not_low, grid.at[first, left], corners.at[3], (west, up)),
    ]
    for k in range(1, faces):
        to = (lax.rem(s + k, faces), t)
        plan.append((t == 0, t == 0, grid.at[first], polar.at[s], to))
    for k in range(1, faces):
        to = (lax.rem(s + k, faces), t)
        plan.append((t == tiles - 1, t == tiles - 1, grid.at[last], polar.at[s], to))
    return plan


def guarded(cond, action):
    if cond is None:
        action()
    else:
        pl.when(cond)(action)


def start_halo(plan, send_sem, recv_sem):
    copies = []
    for i, (sends, receives, src, dst, to) in enumerate(plan):
        copy = pltpu.make_async_remote_copy(
            src_ref=src, dst_ref=dst, send_sem=send_sem.at[i], recv_sem=recv_sem.at[i],
            device_id=to, device_id_type=MESH,
        )
        guarded(sends, copy.start)
        copies.append((sends, receives, copy))
    return copies


def wait_halo(copies):
    for sends, receives, copy in copies:
        guarded(sends, copy.wait_send)
        guarded(receives, copy.wait_recv)


def own_polar(grid, polar, d, tiles, sem):
    s, t = lax.axis_index("face"), lax.axis_index("tile")
    top = pltpu.make_async_copy(grid.at[pl.ds(0, d)], polar.at[s], sem)
    low = pltpu.make_async_copy(grid.at[pl.ds(grid.shape[0] - d, d)], polar.at[s], sem)
    return [(t == 0, top), (t == tiles - 1, low)]


def first_exchange_kernel(
    faces, tiles, d, grid, pw, pe, rows, cells,
    hw, he, north, south, corners, polar, rows_in, cells_in,
    send_sem, recv_sem, row_send, row_recv, cell_send, cell_recv, own_sem,
):
    count = faces * tiles
    me = lax.axis_index("face") * tiles + lax.axis_index("tile")
    barrier = pltpu.get_barrier_semaphore()

    def device(k):
        other = lax.rem(me + k, count)
        return other, (other // tiles, lax.rem(other, tiles))

    def greet(k, carry):
        _, to = device(k)
        pl.semaphore_signal(barrier, inc=1, device_id=to, device_id_type=MESH)
        return carry

    lax.fori_loop(1, count, greet, 0)
    own_rows = pltpu.make_async_copy(rows.at[me], rows_in.at[me], own_sem.at[0])
    own_cells = pltpu.make_async_copy(cells.at[me], cells_in.at[me], own_sem.at[1])
    own_rows.start()
    own_cells.start()
    own = own_polar(grid, polar, d, tiles, own_sem.at[2])
    for cond, copy in own:
        guarded(cond, copy.start)
    pl.semaphore_wait(barrier, count - 1)
    copies = start_halo(
        halo_sends(faces, tiles, d, grid, pw, pe, hw, he, north, south, corners, polar), send_sem, recv_sem
    )

    def row_copy(k):
        other, to = device(k)
        return pltpu.make_async_remote_copy(
            src_ref=rows.at[other], dst_ref=rows_in.at[me],
            send_sem=row_send.at[k], recv_sem=row_recv.at[k], device_id=to, device_id_type=MESH,
        )

    def cell_copy(k):
        other, to = device(k)
        return pltpu.make_async_remote_copy(
            src_ref=cells.at[other], dst_ref=cells_in.at[me],
            send_sem=cell_send.at[k], recv_sem=cell_recv.at[k], device_id=to, device_id_type=MESH,
        )

    def send(k, carry):
        row_copy(k).start()
        cell_copy(k).start()
        return carry

    def finish(k, carry):
        row_copy(k).wait()
        cell_copy(k).wait()
        return carry

    lax.fori_loop(1, count, send, 0)
    wait_halo(copies)
    for cond, copy in own:
        guarded(cond, copy.wait)
    own_rows.wait()
    own_cells.wait()
    lax.fori_loop(1, count, finish, 0)


def second_exchange_kernel(
    faces, tiles, d, grid, pw, pe, hw, he, north, south, corners, polar, send_sem, recv_sem, own_sem
):
    s, t = lax.axis_index("face"), lax.axis_index("tile")
    barrier = pltpu.get_barrier_semaphore()

    def greet(to):
        pl.semaphore_signal(barrier, inc=1, device_id=to, device_id_type=MESH)

    east, west = lax.rem(s + 1, faces), lax.rem(s + faces - 1, faces)
    greet((east, t))
    greet((west, t))

    @pl.when(t > 0)
    def _():
        for f in (east, s, west):
            greet((f, t - 1))

    @pl.when(t < tiles - 1)
    def _():
        for f in (east, s, west):
            greet((f, t + 1))

    polar_end = (t == 0) | (t == tiles - 1)

    @pl.when(polar_end)
    def _():
        for k in range(2, faces - 1):
            greet((lax.rem(s + k, faces), t))

    own = own_polar(grid, polar, d, tiles, own_sem.at[0])
    for cond, copy in own:
        guarded(cond, copy.start)

    @pl.when(polar_end)
    def _():
        pl.semaphore_wait(barrier, 5 + faces - 3)

    @pl.when(jnp.logical_not(polar_end))
    def _():
        pl.semaphore_wait(barrier, 8)

    copies = start_halo(
        halo_sends(faces, tiles, d, grid, pw, pe, hw, he, north, south, corners, polar), send_sem, recv_sem
    )
    wait_halo(copies)
    for cond, copy in own:
        guarded(cond, copy.wait)


def fill_padded(faces, tiles, d, pad, grid, hw, he, north, south, corners, polar, link, turn):
    s, t = lax.axis_index("face"), lax.axis_index("tile")
    rows, cols = grid.shape[0], grid.shape[1]
    wide = cols + EDGE
    pad[d : d + rows, :cols] = grid[...]
    pad[d : d + rows, cols:] = jnp.concatenate(
        [unpack_columns(he[...], d, False), unpack_columns(hw[...], d, True)], axis=1
    ).astype(jnp.bfloat16)

    def from_pole(base, column):
        p = link[s, column]
        east, west = lax.rem(p + 1, faces), lax.rem(p + faces - 1, faces)
        here = lax.broadcasted_iota(jnp.int32, (wide, wide), 0)
        there = lax.broadcasted_iota(jnp.int32, (wide, wide), 1)
        mirrored = jnp.where(here < cols, cols - 1 - here, wide + cols - 1 - here)
        source = jnp.where(turn[s, column] == 1, mirrored, here)
        move = jnp.where(there == source, 1.0, 0.0).astype(jnp.bfloat16)
        for i in range(d):
            k = d - 1 - i
            edge = join_edge(polar[east, k, :EDGE], polar[west, k, cols - EDGE :])
            line = jnp.concatenate([polar[p, k], edge], axis=0)
            pad[base + i] = jnp.dot(move, line, preferred_element_type=jnp.float32).astype(jnp.bfloat16)

    @pl.when(t == 0)
    def _():
        from_pole(0, 0)

    @pl.when(t > 0)
    def _():
        pad[:d, :cols] = north[...]
        pad[:d, cols:] = join_edge(corners[1], corners[0])

    @pl.when(t == tiles - 1)
    def _():
        from_pole(d + rows, 1)

    @pl.when(t < tiles - 1)
    def _():
        pad[d + rows :, :cols] = south[...]
        pad[d + rows :, cols:] = join_edge(corners[3], corners[2])


def fill_taps(taps, wide_taps):
    channels, features = taps.shape[1], taps.shape[2]
    for a in range(3):
        for e in range(3):
            wide_taps[a * channels : (a + 1) * channels, e * features : (e + 1) * features] = taps[3 * a + e]


def conv_rows(pad, wide_taps, bias, d, start, count, cols):
    wide = cols + EDGE
    features = bias.shape[-1]
    lines = [
        pad[pl.ds(start + a * d, count)].reshape(count * wide, pad.shape[-1]) for a in range(3)
    ]
    product = jnp.dot(
        jnp.concatenate(lines, axis=1), wide_taps[...], preferred_element_type=jnp.float32
    ).reshape(count, wide, 3 * features)
    low = pltpu.roll(product[:, :, :features], d, 1)
    high = pltpu.roll(product[:, :, 2 * features :], wide - d, 1)
    total = low + product[:, :, features : 2 * features] + high
    return total[:, :cols] + bias[...].reshape(1, 1, features)


def first_compute_kernel(
    faces, tiles, d, d_next, step_rows,
    link, turn, cells, grid, hw, he, north, south, corners, polar, taps, bias, values, weight,
    mixed, pw_out, pe_out, pad, wide_taps, inject, encoded,
):
    rows, cols = grid.shape[0], grid.shape[1]
    sources, slots, features = values.shape
    channels = bias.shape[-1]
    cell_total = rows * cols
    fill_taps(taps, wide_taps)
    encoded[...] = jnp.dot(
        values[...].reshape(sources * slots, features), weight[...], preferred_element_type=jnp.float32
    )
    inject[...] = jnp.zeros_like(inject)
    fill_padded(faces, tiles, d, pad, grid, hw, he, north, south, corners, polar, link, turn)
    group = 8

    def add_group(i, carry):
        source, at = i // (slots // group), lax.rem(i, slots // group) * group

        @pl.when(cells[source, at] < cell_total)
        def _():
            chunk = encoded[pl.ds(pl.multiple_of(i * group, group), group)]
            for j in range(group):
                place = cells[source, at + j]
                inject[pl.ds(place, 1)] += chunk[j : j + 1]

        return carry

    lax.fori_loop(0, sources * slots // group, add_group, 0)

    def step(i, carry):
        start = i * step_rows
        first = jax.nn.gelu(
            conv_rows(pad, wide_taps, bias, d, start, step_rows, cols), approximate=True
        )
        at = pl.multiple_of(start * cols, step_rows * cols)
        added = inject[pl.ds(at, step_rows * cols)].reshape(step_rows, cols, channels)
        mixed[pl.ds(start, step_rows)] = (first + added).astype(jnp.bfloat16)
        return carry

    lax.fori_loop(0, rows // step_rows, step, 0)
    pw_out[...] = pack_columns(mixed[:, :EDGE].astype(jnp.float32), d_next, False)
    pe_out[...] = pack_columns(mixed[:, cols - EDGE :].astype(jnp.float32), d_next, True)


def second_compute_kernel(
    faces, tiles, d, step_rows,
    link, turn, grid, hw, he, north, south, corners, polar, taps, bias, fields,
    out, pad, wide_taps,
):
    rows, cols = grid.shape[0], grid.shape[1]
    fill_taps(taps, wide_taps)
    fill_padded(faces, tiles, d, pad, grid, hw, he, north, south, corners, polar, link, turn)

    def step(i, carry):
        start = i * step_rows
        second = jax.nn.gelu(
            conv_rows(pad, wide_taps, bias, d, start, step_rows, cols), approximate=True
        )
        here = fields[pl.ds(start, step_rows)].astype(jnp.float32)
        out[pl.ds(start, step_rows)] = (here + second).astype(jnp.bfloat16)
        return carry

    lax.fori_loop(0, rows // step_rows, step, 0)


def local(
    fields, first_kernel_taps, first_conv_bias, second_kernel_taps, second_conv_bias,
    obs_weight, obs_values, obs_owner, obs_cells, polar_neighbor_sector, polar_link_reversal,
):
    faces, tiles = lax.axis_size("face"), lax.axis_size("tile")
    rows, cols, channels = fields.shape
    obs_rows, features = obs_values.shape
    dest_count = faces * tiles
    slots = 2 * obs_rows // dest_count
    cell_total = rows * cols
    step_rows = 4
    bf16, f32, i32 = jnp.bfloat16, jnp.float32, jnp.int32
    shape = jax.ShapeDtypeStruct
    vmem = pl.BlockSpec(memory_space=pltpu.VMEM)
    smem = pl.BlockSpec(memory_space=pltpu.SMEM)
    anywhere = pl.BlockSpec(memory_space=pl.ANY)
    params = pltpu.CompilerParams(vmem_limit_bytes=VMEM_LIMIT)

    def packed_shape(d):
        return shape((rows * d // EDGE, EDGE, channels), bf16)

    def halo_shapes(d):
        return [
            packed_shape(d), packed_shape(d),
            shape((d, cols, channels), bf16), shape((d, cols, channels), bf16),
            shape((4, d, EDGE, channels), bf16), shape((faces, d, cols, channels), bf16),
        ]

    halo_copies = 8 + 2 * (faces - 1)
    dma = pltpu.SemaphoreType.DMA
    d1, d2 = FIRST_DILATION, SECOND_DILATION

    def edge_block(index):
        return pl.BlockSpec((rows, EDGE, channels), lambda i: (0, index, 0))

    whole = lambda *dims: pl.BlockSpec(dims, lambda i: (0,) * len(dims))
    send_rows, send_cells, pw, pe = pl.pallas_call(
        functools.partial(pack_kernel, dest_count, slots, cell_total, d1),
        grid=(1,),
        out_shape=[
            shape((dest_count, slots, features), bf16), shape((dest_count, 1, LANES), i32),
            packed_shape(d1), packed_shape(d1),
        ],
        in_specs=[
            whole(1, obs_rows), whole(1, obs_rows), whole(obs_rows, features),
            edge_block(0), edge_block(cols // EDGE - 1),
        ],
        out_specs=[
            whole(dest_count, slots, features), whole(dest_count, 1, LANES),
            whole(*packed_shape(d1).shape), whole(*packed_shape(d1).shape),
        ],
        compiler_params=params,
        name="pack_observations",
    )(obs_owner.reshape(1, obs_rows), obs_cells.reshape(1, obs_rows), obs_values, fields, fields)

    *halo, recv_rows, recv_cells = pl.pallas_call(
        functools.partial(first_exchange_kernel, faces, tiles, d1),
        out_shape=halo_shapes(d1) + [
            shape((dest_count, slots, features), bf16), shape((dest_count, 1, LANES), i32),
        ],
        in_specs=[anywhere] * 5,
        out_specs=[anywhere] * 8,
        scratch_shapes=[
            dma((halo_copies,)), dma((halo_copies,)), dma((dest_count,)), dma((dest_count,)),
            dma((dest_count,)), dma((dest_count,)), dma((3,)),
        ],
        compiler_params=pltpu.CompilerParams(collective_id=0, has_side_effects=True),
        name="first_exchange",
    )(fields, pw, pe, send_rows, send_cells)

    mixed, pw, pe = pl.pallas_call(
        functools.partial(first_compute_kernel, faces, tiles, d1, d2, step_rows),
        out_shape=[shape((rows, cols, channels), bf16), packed_shape(d2), packed_shape(d2)],
        in_specs=[smem] * 3 + [vmem] * 11,
        out_specs=[vmem] * 3,
        scratch_shapes=[
            pltpu.VMEM((rows + 2 * d1, cols + EDGE, channels), bf16),
            pltpu.VMEM((3 * channels, 3 * channels), bf16),
            pltpu.VMEM((cell_total + 8, channels), f32),
            pltpu.VMEM((dest_count * slots, channels), f32),
        ],
        compiler_params=params,
        name="first_compute",
    )(
        polar_neighbor_sector, polar_link_reversal, recv_cells.reshape(dest_count, LANES),
        fields, *halo, first_kernel_taps, first_conv_bias.reshape(1, channels), recv_rows, obs_weight,
    )

    halo = pl.pallas_call(
        functools.partial(second_exchange_kernel, faces, tiles, d2),
        out_shape=halo_shapes(d2),
        in_specs=[anywhere] * 3,
        out_specs=[anywhere] * 6,
        scratch_shapes=[dma((halo_copies,)), dma((halo_copies,)), dma((1,))],
        compiler_params=pltpu.CompilerParams(collective_id=1, has_side_effects=True),
        name="second_exchange",
    )(mixed, pw, pe)

    return pl.pallas_call(
        functools.partial(second_compute_kernel, faces, tiles, d2, step_rows),
        out_shape=shape((rows, cols, channels), bf16),
        in_specs=[smem] * 2 + [vmem] * 10,
        out_specs=vmem,
        scratch_shapes=[
            pltpu.VMEM((rows + 2 * d2, cols + EDGE, channels), bf16),
            pltpu.VMEM((3 * channels, 3 * channels), bf16),
        ],
        compiler_params=params,
        name="second_compute",
    )(
        polar_neighbor_sector, polar_link_reversal,
        mixed, *halo, second_kernel_taps, second_conv_bias.reshape(1, channels), fields,
    )


def solution(mesh):
    in_specs = (
        P("tile", "face", None), P(), P(), P(), P(), P(),
        P(("face", "tile"), None), P(("face", "tile"), None), P(("face", "tile")), P(), P(),
    )
    return jax.shard_map(
        local, mesh=mesh, in_specs=in_specs, out_specs=P("tile", "face", None), check_vma=False
    )
```

time: 225 us -> 86.2 us (0.38)
  Pallas kernels: 0 us -> 82.7 us
  matrix products: 60 us -> 0 us
  blocking collectives: 57.9 us -> 0 us
  other arithmetic: 37.4 us -> 0 us
  starting transfers between devices: 29 us -> 0 us
  local copies, waits for them, and re-layouts: 31.1 us -> 2.69 us
  between operations: 6.99 us -> 0.02 us
    pallas_call x0 -> x5, Pallas kernels: none -> 82.7 us  [the longest x1 26 us: local(): pl.pallas_call(functools.partial(first_compute_kernel, faces, tiles, d1,...]
    dot_general x34 -> x0, matrix products: 60 us -> none  [the longest x18 25.9 us: apply_stencil_taps(): jnp.dot(window.reshape(rows * cols, channels), kernel[tap_row * 3 + tap_c...]
    all_gather x4 -> x0, blocking collectives: 57.9 us -> none  [the longest x2 29.6 us: pad_sector_halo(): lax.all_gather(bottom_rows, 'face', axis=0, tiled=True)]
    ppermute x8 -> x0, starting transfers between devices: 18.9 us -> none  [the longest x4 12.1 us: padded_2(): lax.ppermute(lax.slice_in_dim(block, block.shape[dim] - width, None, axis...]
    concatenate x6 -> x0, other arithmetic: 17.5 us -> none  [the longest x2 8.96 us: pad_sector_halo(): jnp.concatenate([upper, tall[dilation:total_rows - dilation], lower], axi...]
    all_to_all x2 -> x0, starting transfers between devices: 10 us -> none  [the longest x1 5.84 us: local(): lax.all_to_all(direct_rows, ('face', 'tile'), split_axis=0, concat_axis=0...]
    dynamic_slice x18 -> x0, local copies, waits for them, and re-layouts: 8.64 us -> none  [the longest x9 5.24 us: local(): lax.map(gather_cells, cell_bases).reshape(cell_total, feature_count)]
    add x16 -> x0, other arithmetic: 8.28 us -> none  [the longest x9 5.82 us: gather_cells(): wanted = base + jnp.arange(cell_block, dtype=jnp.int32)]
  transfers between devices with their start and end apart: 10 -> 0, of which waited for: 0 -> 0; matrix products, arithmetic and copies ran while one was open for 30% -> 0% of each run, Pallas kernels for 0% -> 0%
where the time goes in v1:
time: 86.2 us; the launch traced here: 85.5 us
  Pallas kernels  82.7 us (96%)
  local copies, waits for them, and re-layouts  2.69 us (3%)
    pallas_call x1, Pallas kernels, local(): pl.pallas_call(functools.partial(first_compute_kernel, faces, tiles, d1,...  26 us
    pallas_call x1, Pallas kernels, local(): pl.pallas_call(functools.partial(first_exchange_kernel, faces, tiles, d1)...  22.7 us
    pallas_call x1, Pallas kernels, local(): pl.pallas_call(functools.partial(second_compute_kernel, faces, tiles, d2,...  15.1 us
    pallas_call x1, Pallas kernels, local(): pl.pallas_call(functools.partial(second_exchange_kernel, faces, tiles, d2...  14.2 us
    pallas_call x1, Pallas kernels, local(): pl.pallas_call(functools.partial(pack_kernel, dest_count, slots, cell_tot...  4.75 us
    unnamed x2, local copies, waits for them, and re-layouts  2.69 us

profile of v1, /device:TPU:0, one launch (start us, length us, event | category | flops | bytes accessed | tf_op | source)
XLA Modules:
  0.0 85.5 jit_solution(2988671756815542087)
XLA Ops:
  0.0 1.4 %copy.14.link = s32[4,2]{1,0:T(4,128)} copy(s32[4,2]{0,1:T(2,128)} %param.20) | data formatting | bytes 64 | tf_op args[9]
  1.4 1.3 %copy.15.turn = s32[4,2]{1,0:T(4,128)} copy(s32[4,2]{0,1:T(2,128)} %param.21) | data formatting | bytes 64 | tf_op args[10]
  2.7 4.7 %pack_observations.1 = (bf16[32,64,128]{2,1,0:T(8,128)(2,1)}, s32[32,1,128]{2,1,0:T(1,128)}, bf16[12,16,128]{2,1,0:T(8,128)(2,1)}, bf16[12,16,128]{2,1,0:T(8,128)(2,1)}) custom-call(s32[1,1024]{1,0:T(1,128)} %bitcast.6, s32[1,1024]{1,0:T(1,128)} %bitcast.7, bf16[1024,128]{1,0:T(8,128)(2,1)} %values_ref.1, bf16[96,96,128]{2,1,0:T(8,128)(2,1)} %fields.1, ...), custom_call_target="tpu_custom_call" | custom-call | tf_op jit(solution)/shard_map/pack_observations/pallas_call | solution.py:437
  7.4 22.7 %first_exchange.1 = (bf16[12,16,128]{2,1,0:T(8,128)(2,1)}, bf16[12,16,128]{2,1,0:T(8,128)(2,1)}, bf16[2,96,128]{2,1,0:T(8,128)(2,1)}, bf16[2,96,128]{2,1,0:T(8,1...) custom-call(bf16[96,96,128]{2,1,0:T(8,128)(2,1)} %fields.1, ...), custom_call_target="tpu_custom_call" | custom-call | tf_op jit(solution)/shard_map/first_exchange/pallas_call | solution.py:456
  30.1 26.0 %first_compute.1 = (bf16[96,96,128]{2,1,0:T(8,128)(2,1)}, bf16[24,16,128]{2,1,0:T(8,128)(2,1)}, bf16[24,16,128]{2,1,0:T(8,128)(2,1)}) custom-call(s32[4,2]{1,0:T(4,128)} %copy.14.link, s32[4,2]{1,0:T(4,128)} %copy.15.turn, s32[32,128]{1,0:T(8,128)} %bitcast.5, bf16[96,96,128]{2,1,0:T(8,128)(2,1)} %fields.1, bf16[12,16,128]{2,1,0:T(8,128)(2,1)} %get-tuple-element.31.hw, ...), custom_call_target="tpu_custom_call" | custom-call | tf_op jit(solution)/shard_map/first_compute/pallas_call | solution.py:471
  56.1 14.2 %second_exchange.1 = (bf16[24,16,128]{2,1,0:T(8,128)(2,1)}, bf16[24,16,128]{2,1,0:T(8,128)(2,1)}, bf16[4,96,128]{2,1,0:T(8,128)(2,1)}, bf16[4,96,128]{2,1,0:T(8,...) custom-call(bf16[96,96,128]{2,1,0:T(8,128)(2,1)} %get-tuple-element.38.grid, ...), custom_call_target="tpu_custom_call" | custom-call | tf_op jit(solution)/shard_map/second_exchange/pallas_call | solution.py:489
  70.3 15.1 %second_compute.1 = bf16[96,96,128]{2,1,0:T(8,128)(2,1)} custom-call(s32[4,2]{1,0:T(4,128)} %copy.14.link, s32[4,2]{1,0:T(4,128)} %copy.15.turn, bf16[96,96,128]{2,1,0:T(8,128)(2,1)} %get-tuple-element.38.grid, bf16[24,16,128]{2,1,0:T(8,128)(2,1)} %get-tuple-element.41.hw, bf16[24,16,128]{2,1,0:T(8,128)(2,1)} %get-tuple-element.42.he, ...), custom_call_target="tpu_custom_call" | custom-call | tf_op jit(solution)/shard_map/second_compute/pallas_call | solution.py:499

commit v2 on v1

v2 whole, which is shorter than its diff:
```python
import functools

import jax
import jax.numpy as jnp
from jax import lax
from jax.experimental import pallas as pl
from jax.experimental.pallas import tpu as pltpu
from jax.sharding import PartitionSpec as P

FIRST_DILATION = 2
SECOND_DILATION = 4
MESH = pl.DeviceIdType.MESH
LANES = 128
EDGE = 16
STEP = 8
VMEM_LIMIT = 56 * 1024 * 1024


def pack_columns(tile, d, east):
    rows, _, ch = tile.shape
    per = 8 // d
    half = tile[:, 8:] if east else tile[:, :8]
    grouped = half.reshape(rows // per, per, 8, ch)
    sub = lax.broadcasted_iota(jnp.int32, (rows // per, 8, ch), 1)
    out = None
    for j in range(per):
        shift = (j * d - (8 - d if east else 0)) % 8
        part = grouped[:, j]
        if shift:
            part = pltpu.roll(part, shift, 1)
        out = part if out is None else jnp.where(sub >= j * d, part, out)
    return out.reshape(rows // (2 * per), EDGE, ch).astype(jnp.bfloat16)


def unpack_columns(packed, d, west):
    count, _, ch = packed.shape
    per = 8 // d
    pieces = packed.astype(jnp.float32).reshape(2 * count, 8, ch)
    parts = []
    for j in range(per):
        shift = ((8 - d if west else 0) - j * d) % 8
        parts.append(pltpu.roll(pieces, shift, 1) if shift else pieces)
    return jnp.stack(parts, axis=1).reshape(2 * count * per, 8, ch)


def join_edge(east_tile, west_tile):
    east = east_tile.astype(jnp.float32)
    west = west_tile.astype(jnp.float32)
    axis = east.ndim - 2
    return jnp.concatenate(
        [lax.slice_in_dim(east, 0, 8, axis=axis), lax.slice_in_dim(west, 8, 16, axis=axis)], axis=axis
    ).astype(jnp.bfloat16)


def pack_observations(dest_count, slots, cell_total, owner_ref, cells_ref, values_ref, rows_out, cells_out):
    obs = owner_ref.shape[1]
    owner = owner_ref[...]
    dests = lax.broadcasted_iota(jnp.int32, (dest_count, obs), 0)
    onehot = jnp.where(dests == owner, 1.0, 0.0)
    before = (
        lax.broadcasted_iota(jnp.int32, (obs, obs), 0) < lax.broadcasted_iota(jnp.int32, (obs, obs), 1)
    )
    ranks = jnp.dot(
        onehot.astype(jnp.bfloat16),
        jnp.where(before, 1.0, 0.0).astype(jnp.bfloat16),
        preferred_element_type=jnp.float32,
    )
    rank = jnp.sum(ranks * onehot, axis=0, keepdims=True).astype(jnp.int32)
    target = owner * slots + rank
    cells = cells_ref[...]
    kind = lax.broadcasted_iota(jnp.int32, (8, obs), 0)
    codes = jnp.where(kind == 0, cells >> 7, jnp.where(kind == 1, cells & 127, 1))
    codes = codes.astype(jnp.float32).astype(jnp.bfloat16)
    values = values_ref[...]
    cells_out[...] = jnp.full(cells_out.shape, cell_total, jnp.int32)
    block = min(512, dest_count * slots)
    for base in range(0, dest_count * slots, block):
        wanted = base + lax.broadcasted_iota(jnp.int32, (block, obs), 0)
        match = jnp.where(wanted == target, 1.0, 0.0).astype(jnp.bfloat16)
        rows = jnp.dot(match, values, preferred_element_type=jnp.float32).astype(jnp.bfloat16)
        first = base // slots
        rows_out[first : first + block // slots] = rows.reshape(block // slots, slots, rows.shape[-1])
        got = lax.dot_general(
            codes, match, (((1,), (1,)), ((), ())), preferred_element_type=jnp.float32
        )
        found = (got[0:1] * LANES + got[1:2]).astype(jnp.int32)
        found = jnp.where(got[2:3] > 0.5, found, cell_total)
        for j in range(block // slots):
            cells_out[first + j, :, :slots] = found[:, j * slots : (j + 1) * slots]


def halo_sends(faces, tiles, d, grid, pw, pe, hw, he, north, south, corners, polar):
    s, t = lax.axis_index("face"), lax.axis_index("tile")
    rows, cols = grid.shape[0], grid.shape[1]
    east, west = lax.rem(s + 1, faces), lax.rem(s + faces - 1, faces)
    last, first = pl.ds(rows - d, d), pl.ds(0, d)
    right, left = pl.ds(cols - EDGE, EDGE), pl.ds(0, EDGE)
    not_top, not_low = t > 0, t < tiles - 1
    up, down = t - 1, t + 1
    plan = [
        (None, None, pe, hw, (east, t)),
        (None, None, pw, he, (west, t)),
        (not_low, not_top, grid.at[last], north, (s, down)),
        (not_top, not_low, grid.at[first], south, (s, up)),
        (not_low, not_top, grid.at[last, right], corners.at[0], (east, down)),
        (not_low, not_top, grid.at[last, left], corners.at[1], (west, down)),
        (not_top, not_low, grid.at[first, right], corners.at[2], (east, up)),
        (not_top, not_low, grid.at[first, left], corners.at[3], (west, up)),
    ]
    for k in range(1, faces):
        to = (lax.rem(s + k, faces), t)
        plan.append((t == 0, t == 0, grid.at[first], polar.at[s], to))
    for k in range(1, faces):
        to = (lax.rem(s + k, faces), t)
        plan.append((t == tiles - 1, t == tiles - 1, grid.at[last], polar.at[s], to))
    return plan


def guarded(cond, action):
    if cond is None:
        action()
    else:
        pl.when(cond)(action)


def start_halo(plan, send_sem, recv_sem):
    copies = []
    for i, (sends, receives, src, dst, to) in enumerate(plan):
        copy = pltpu.make_async_remote_copy(
            src_ref=src, dst_ref=dst, send_sem=send_sem.at[i], recv_sem=recv_sem.at[i],
            device_id=to, device_id_type=MESH,
        )
        guarded(sends, copy.start)
        copies.append((sends, receives, copy))
    return copies


def wait_received(copies):
    for _, receives, copy in copies:
        guarded(receives, copy.wait_recv)


def wait_sent(copies):
    for sends, _, copy in copies:
        guarded(sends, copy.wait_send)


def own_polar(grid, polar, d, tiles, sem):
    s, t = lax.axis_index("face"), lax.axis_index("tile")
    top = pltpu.make_async_copy(grid.at[pl.ds(0, d)], polar.at[s], sem)
    low = pltpu.make_async_copy(grid.at[pl.ds(grid.shape[0] - d, d)], polar.at[s], sem)
    return [(t == 0, top), (t == tiles - 1, low)]


def fill_columns(d, pad, rows, cols, hw, he):
    pad[d : d + rows, cols:] = jnp.concatenate(
        [unpack_columns(he[...], d, False), unpack_columns(hw[...], d, True)], axis=1
    ).astype(jnp.bfloat16)


def fill_ends(faces, tiles, d, pad, rows, cols, north, south, corners, polar, link, turn):
    s, t = lax.axis_index("face"), lax.axis_index("tile")
    wide = cols + EDGE

    def from_pole(base, column):
        p = link[column, s]
        east, west = lax.rem(p + 1, faces), lax.rem(p + faces - 1, faces)
        here = lax.broadcasted_iota(jnp.int32, (wide, wide), 0)
        there = lax.broadcasted_iota(jnp.int32, (wide, wide), 1)
        mirrored = jnp.where(here < cols, cols - 1 - here, wide + cols - 1 - here)
        source = jnp.where(turn[column, s] == 1, mirrored, here)
        move = jnp.where(there == source, 1.0, 0.0).astype(jnp.bfloat16)
        for i in range(d):
            k = d - 1 - i
            edge = join_edge(polar[east, k, :EDGE], polar[west, k, cols - EDGE :])
            line = jnp.concatenate([polar[p, k], edge], axis=0)
            pad[base + i] = jnp.dot(move, line, preferred_element_type=jnp.float32).astype(jnp.bfloat16)

    @pl.when(t == 0)
    def _():
        from_pole(0, 0)

    @pl.when(t > 0)
    def _():
        pad[:d, :cols] = north[...]
        pad[:d, cols:] = join_edge(corners[1], corners[0])

    @pl.when(t == tiles - 1)
    def _():
        from_pole(d + rows, 1)

    @pl.when(t < tiles - 1)
    def _():
        pad[d + rows :, :cols] = south[...]
        pad[d + rows :, cols:] = join_edge(corners[3], corners[2])


def fill_taps(taps, wide_taps):
    channels, features = taps.shape[1], taps.shape[2]
    for k in range(4):
        for e in range(3):
            for j in range(2):
                piece = (
                    taps[3 * (k - j) + e] if 0 <= k - j <= 2 else jnp.zeros((channels, features), jnp.bfloat16)
                )
                at = (2 * e + j) * features
                wide_taps[k * channels : (k + 1) * channels, at : at + features] = piece


def conv_rows(pad, wide_taps, bias, d, start, cols):
    wide = cols + EDGE
    features = bias.shape[-1]
    count = STEP // (2 * d)
    lines = []
    for k in range(4):
        blocks = [pad[pl.ds(start + m * 2 * d + k * d, d)] for m in range(count)]
        lines.append(jnp.concatenate(blocks, axis=0).reshape(count * d * wide, pad.shape[-1]))
    product = jnp.dot(
        jnp.concatenate(lines, axis=1), wide_taps[...], preferred_element_type=jnp.float32
    ).reshape(count * d, wide, 6 * features)
    halves = []
    for j in range(2):
        low, middle, high = (
            product[:, :, (2 * e + j) * features : (2 * e + j + 1) * features] for e in range(3)
        )
        total = pltpu.roll(low, d, 1) + middle + pltpu.roll(high, wide - d, 1)
        halves.append(total[:, :cols] + bias[...].reshape(1, 1, features))
    return [(m * 2 * d + j * d, halves[j][m * d : (m + 1) * d]) for m in range(count) for j in range(2)]


def first_kernel(
    faces, tiles, d, slots,
    link, turn, owner, cells, values, taps, bias, grid,
    first, rows_in, cells_in,
    pad, wide_taps, held, rows_out, cells_out, pw, pe, hw, he, north, south, corners, polar,
    send_sem, recv_sem, row_send, row_recv, cell_send, cell_recv, own_sem,
):
    rows, cols, channels = grid.shape
    cell_total = rows * cols
    count = faces * tiles
    me = lax.axis_index("face") * tiles + lax.axis_index("tile")
    barrier = pltpu.get_barrier_semaphore()
    load = pltpu.make_async_copy(grid, pad.at[pl.ds(d, rows), pl.ds(0, cols)], own_sem.at[3])
    load.start()

    def device(k):
        other = lax.rem(me + k, count)
        return other, (other // tiles, lax.rem(other, tiles))

    def greet(k, carry):
        _, to = device(k)
        pl.semaphore_signal(barrier, inc=1, device_id=to, device_id_type=MESH)
        return carry

    lax.fori_loop(1, count, greet, 0)
    own = own_polar(grid, polar, d, tiles, own_sem.at[2])
    for cond, copy in own:
        guarded(cond, copy.start)
    load.wait()
    pw[...] = pack_columns(pad[d : d + rows, :EDGE].astype(jnp.float32), d, False)
    pe[...] = pack_columns(pad[d : d + rows, cols - EDGE : cols].astype(jnp.float32), d, True)
    pl.semaphore_wait(barrier, count - 1)
    copies = start_halo(
        halo_sends(faces, tiles, d, grid, pw, pe, hw, he, north, south, corners, polar), send_sem, recv_sem
    )

    pack_observations(count, slots, cell_total, owner, cells, values, rows_out, cells_out)

    def row_copy(k):
        other, to = device(k)
        return pltpu.make_async_remote_copy(
            src_ref=rows_out.at[other], dst_ref=rows_in.at[me],
            send_sem=row_send.at[k], recv_sem=row_recv.at[k], device_id=to, device_id_type=MESH,
        )

    def cell_copy(k):
        other, to = device(k)
        return pltpu.make_async_remote_copy(
            src_ref=cells_out.at[other], dst_ref=cells_in.at[me],
            send_sem=cell_send.at[k], recv_sem=cell_recv.at[k], device_id=to, device_id_type=MESH,
        )

    def send(k, carry):
        row_copy(k).start()
        cell_copy(k).start()
        return carry

    def finish(k, carry):
        row_copy(k).wait()
        cell_copy(k).wait()
        return carry

    lax.fori_loop(1, count, send, 0)
    own_rows = pltpu.make_async_copy(rows_out.at[me], rows_in.at[me], own_sem.at[0])
    own_cells = pltpu.make_async_copy(cells_out.at[me], cells_in.at[me], own_sem.at[1])
    own_rows.start()
    own_cells.start()

    fill_taps(taps, wide_taps)
    wait_received(copies[:2])
    fill_columns(d, pad, rows, cols, hw, he)

    def step(i, carry):
        start = i * STEP
        for offset, piece in conv_rows(pad, wide_taps, bias, d, start, cols):
            at = pl.multiple_of((start + offset) * cols, d * cols)
            held[pl.ds(at, d * cols)] = jax.nn.gelu(piece, approximate=True).reshape(d * cols, channels)
        return carry

    steps = rows // STEP
    lax.fori_loop(1, steps - 1, step, 0, unroll=2)
    wait_received(copies[2:])
    for cond, copy in own:
        guarded(cond, copy.wait)
    fill_ends(faces, tiles, d, pad, rows, cols, north, south, corners, polar, link, turn)
    step(0, 0)
    step(steps - 1, 0)
    store = pltpu.make_async_copy(held, first, own_sem.at[4])
    store.start()
    wait_sent(copies)
    own_rows.wait()
    own_cells.wait()
    lax.fori_loop(1, count, finish, 0)
    store.wait()


def inject_kernel(d_next, cells, first, values, weight, mixed, pw_out, pe_out, total, encoded, sem):
    rows, cols, channels = mixed.shape
    sources, slots, features = values.shape
    cell_total = rows * cols
    load = pltpu.make_async_copy(first, total.at[pl.ds(0, cell_total)], sem)
    load.start()
    encoded[...] = jnp.dot(
        values[...].reshape(sources * slots, features), weight[...], preferred_element_type=jnp.float32
    )
    total[cell_total:] = jnp.zeros((total.shape[0] - cell_total, channels), jnp.float32)
    load.wait()
    group = 8

    def add_group(i, carry):
        source, at = i // (slots // group), lax.rem(i, slots // group) * group

        @pl.when(cells[source, at] < cell_total)
        def _():
            chunk = encoded[pl.ds(pl.multiple_of(i * group, group), group)]
            for j in range(group):
                place = cells[source, at + j]
                total[pl.ds(place, 1)] += chunk[j : j + 1]

        return carry

    lax.fori_loop(0, sources * slots // group, add_group, 0)

    def step(i, carry):
        at = pl.multiple_of(i * STEP * cols, STEP * cols)
        here = total[pl.ds(at, STEP * cols)].reshape(STEP, cols, channels)
        mixed[pl.ds(i * STEP, STEP)] = here.astype(jnp.bfloat16)
        return carry

    lax.fori_loop(0, rows // STEP, step, 0)
    pw_out[...] = pack_columns(mixed[:, :EDGE].astype(jnp.float32), d_next, False)
    pe_out[...] = pack_columns(mixed[:, cols - EDGE :].astype(jnp.float32), d_next, True)


def second_kernel(
    faces, tiles, d, link, turn, taps, bias, grid, pw, pe, fields,
    out,
    pad, wide_taps, held, hw, he, north, south, corners, polar, send_sem, recv_sem, own_sem,
):
    rows, cols, channels = grid.shape
    s, t = lax.axis_index("face"), lax.axis_index("tile")
    barrier = pltpu.get_barrier_semaphore()

    def greet(to):
        pl.semaphore_signal(barrier, inc=1, device_id=to, device_id_type=MESH)

    east, west = lax.rem(s + 1, faces), lax.rem(s + faces - 1, faces)
    greet((east, t))
    greet((west, t))

    @pl.when(t > 0)
    def _():
        for f in (east, s, west):
            greet((f, t - 1))

    @pl.when(t < tiles - 1)
    def _():
        for f in (east, s, west):
            greet((f, t + 1))

    polar_end = (t == 0) | (t == tiles - 1)

    @pl.when(polar_end)
    def _():
        for k in range(2, faces - 1):
            greet((lax.rem(s + k, faces), t))

    own = own_polar(grid, polar, d, tiles, own_sem.at[0])
    for cond, copy in own:
        guarded(cond, copy.start)
    load = pltpu.make_async_copy(grid, pad.at[pl.ds(d, rows), pl.ds(0, cols)], own_sem.at[1])
    load.start()
    load_fields = pltpu.make_async_copy(fields, held, own_sem.at[2])
    load_fields.start()

    @pl.when(polar_end)
    def _():
        pl.semaphore_wait(barrier, 5 + faces - 3)

    @pl.when(jnp.logical_not(polar_end))
    def _():
        pl.semaphore_wait(barrier, 8)

    copies = start_halo(
        halo_sends(faces, tiles, d, grid, pw, pe, hw, he, north, south, corners, polar), send_sem, recv_sem
    )
    fill_taps(taps, wide_taps)
    load.wait()
    load_fields.wait()
    wait_received(copies[:2])
    fill_columns(d, pad, rows, cols, hw, he)

    def step(i, carry):
        start = i * STEP
        for offset, piece in conv_rows(pad, wide_taps, bias, d, start, cols):
            here = held[pl.ds(start + offset, d)].astype(jnp.float32)
            out[pl.ds(start + offset, d)] = (
                here + jax.nn.gelu(piece, approximate=True)
            ).astype(jnp.bfloat16)
        return carry

    steps = rows // STEP
    lax.fori_loop(1, steps - 1, step, 0, unroll=2)
    wait_received(copies[2:])
    for cond, copy in own:
        guarded(cond, copy.wait)
    fill_ends(faces, tiles, d, pad, rows, cols, north, south, corners, polar, link, turn)
    step(0, 0)
    step(steps - 1, 0)
    wait_sent(copies)


def local(
    fields, first_kernel_taps, first_conv_bias, second_kernel_taps, second_conv_bias,
    obs_weight, obs_values, obs_owner, obs_cells, polar_neighbor_sector, polar_link_reversal,
):
    faces, tiles = lax.axis_size("face"), lax.axis_size("tile")
    rows, cols, channels = fields.shape
    obs_rows, features = obs_values.shape
    dest_count = faces * tiles
    slots = 2 * obs_rows // dest_count
    cell_total = rows * cols
    bf16, f32, i32 = jnp.bfloat16, jnp.float32, jnp.int32
    shape = jax.ShapeDtypeStruct
    vmem = pl.BlockSpec(memory_space=pltpu.VMEM)
    smem = pl.BlockSpec(memory_space=pltpu.SMEM)
    anywhere = pl.BlockSpec(memory_space=pl.ANY)
    dma = pltpu.SemaphoreType.DMA
    d1, d2 = FIRST_DILATION, SECOND_DILATION
    halo_copies = 8 + 2 * (faces - 1)
    link, turn = polar_neighbor_sector.T, polar_link_reversal.T

    def packed_dims(d):
        return (rows * d // EDGE, EDGE, channels)

    def conv_scratch(d):
        return [
            pltpu.VMEM((rows + 2 * d, cols + EDGE, channels), bf16),
            pltpu.VMEM((4 * channels, 6 * channels), bf16),
        ]

    def halo_scratch(d):
        return [
            pltpu.VMEM(packed_dims(d), bf16), pltpu.VMEM(packed_dims(d), bf16),
            pltpu.VMEM((d, cols, channels), bf16), pltpu.VMEM((d, cols, channels), bf16),
            pltpu.VMEM((4, d, EDGE, channels), bf16), pltpu.VMEM((faces, d, cols, channels), bf16),
        ]

    first, recv_rows, recv_cells = pl.pallas_call(
        functools.partial(first_kernel, faces, tiles, d1, slots),
        out_shape=[
            shape((cell_total, channels), f32),
            shape((dest_count, slots, features), bf16),
            shape((dest_count, 1, LANES), i32),
        ],
        in_specs=[smem] * 2 + [vmem] * 5 + [anywhere],
        out_specs=[anywhere] * 3,
        scratch_shapes=conv_scratch(d1) + [
            pltpu.VMEM((cell_total, channels), f32),
            pltpu.VMEM((dest_count, slots, features), bf16),
            pltpu.VMEM((dest_count, 1, LANES), i32),
            pltpu.VMEM(packed_dims(d1), bf16), pltpu.VMEM(packed_dims(d1), bf16),
        ] + halo_scratch(d1) + [
            dma((halo_copies,)), dma((halo_copies,)), dma((dest_count,)), dma((dest_count,)),
            dma((dest_count,)), dma((dest_count,)), dma((5,)),
        ],
        compiler_params=pltpu.CompilerParams(
            collective_id=0, has_side_effects=True, vmem_limit_bytes=VMEM_LIMIT
        ),
        name="first_conv_and_exchange",
    )(
        link, turn, obs_owner.reshape(1, obs_rows), obs_cells.reshape(1, obs_rows), obs_values,
        first_kernel_taps, first_conv_bias.reshape(1, channels), fields,
    )

    mixed, pw, pe = pl.pallas_call(
        functools.partial(inject_kernel, d2),
        out_shape=[
            shape((rows, cols, channels), bf16), shape(packed_dims(d2), bf16), shape(packed_dims(d2), bf16)
        ],
        in_specs=[smem, anywhere, vmem, vmem],
        out_specs=[vmem] * 3,
        scratch_shapes=[
            pltpu.VMEM((cell_total + 8, channels), f32),
            pltpu.VMEM((dest_count * slots, channels), f32),
            dma,
        ],
        compiler_params=pltpu.CompilerParams(vmem_limit_bytes=VMEM_LIMIT),
        name="inject",
    )(recv_cells.reshape(dest_count, LANES), first, recv_rows, obs_weight)

    return pl.pallas_call(
        functools.partial(second_kernel, faces, tiles, d2),
        out_shape=shape((rows, cols, channels), bf16),
        in_specs=[smem] * 2 + [vmem] * 2 + [anywhere] * 4,
        out_specs=vmem,
        scratch_shapes=conv_scratch(d2) + [pltpu.VMEM((rows, cols, channels), bf16)]
        + halo_scratch(d2) + [dma((halo_copies,)), dma((halo_copies,)), dma((3,))],
        compiler_params=pltpu.CompilerParams(
            collective_id=1, has_side_effects=True, vmem_limit_bytes=VMEM_LIMIT
        ),
        name="second_conv_and_exchange",
    )(
        link, turn, second_kernel_taps, second_conv_bias.reshape(1, channels), mixed, pw, pe, fields
    )


def solution(mesh):
    in_specs = (
        P("tile", "face", None), P(), P(), P(), P(), P(),
        P(("face", "tile"), None), P(("face", "tile"), None), P(("face", "tile")), P(), P(),
    )
    return jax.shard_map(
        local, mesh=mesh, in_specs=in_specs, out_specs=P("tile", "face", None), check_vma=False
    )
```

time: 86.2 us -> 63.7 us (0.74)
  Pallas kernels: 82.7 us -> 60.4 us
    pallas_call x5 -> x3, Pallas kernels: 82.7 us -> 60.4 us  [the longest x1 23.8 us: local(): pl.pallas_call(functools.partial(first_kernel, faces, tiles, d1, slots),...]
    unnamed x2 -> x1, local copies, waits for them, and re-layouts: 2.69 us -> 3.22 us
where the time goes in v2:
time: 63.7 us
  Pallas kernels  60.4 us (95%)
  local copies, waits for them, and re-layouts  3.22 us (5%)
    pallas_call x1, Pallas kernels, local(): pl.pallas_call(functools.partial(first_kernel, faces, tiles, d1, slots),...  23.8 us
    pallas_call x1, Pallas kernels, local(): pl.pallas_call(functools.partial(second_kernel, faces, tiles, d2), out_sh...  23.7 us
    pallas_call x1, Pallas kernels, local(): pl.pallas_call(functools.partial(inject_kernel, d2), out_shape=[shape((ro...  12.9 us
    unnamed x1, local copies, waits for them, and re-layouts  3.22 us

profile of v2, /device:TPU:0, one launch (start us, length us, event | category | flops | bytes accessed | tf_op | source)
XLA Modules:
  0.0 63.7 jit_solution(4980618481747423426)
XLA Ops:
  0.0 23.8 %first_conv_and_exchange.1 = (f32[9216,128]{1,0:T(8,128)}, bf16[32,64,128]{2,1,0:T(8,128)(2,1)}, s32[32,1,128]{2,1,0:T(1,128)}) custom-call(s32[2,4]{1,0:T(2,128)} %bitcast.10, s32[2,4]{1,0:T(2,128)} %bitcast.12, s32[1,1024]{1,0:T(1,128)} %bitcast.8, s32[1,1024]{1,0:T(1,128)} %bitcast.9, bf16[1024,128]{1,0:T(8,128)(2,1)} %values.1, ...), custom_call_target="tpu_custom_call" | custom-call | tf_op jit(solution)/shard_map/first_conv_and_exchange/pallas_call | solution.py:479
  23.8 12.9 %inject.1 = (bf16[96,96,128]{2,1,0:T(8,128)(2,1)}, bf16[24,16,128]{2,1,0:T(8,128)(2,1)}, bf16[24,16,128]{2,1,0:T(8,128)(2,1)}) custom-call(s32[32,128]{1,0:T(8,128)} %bitcast.7, f32[9216,128]{1,0:T(8,128)} %get-tuple-element.12.first, bf16[32,64,128]{2,1,0:T(8,128)(2,1)} %get-tuple-element.13.values, bf16[128,128]{1,0:T(8,128)(2,1)} %weight.1), custom_call_target="tpu_custom_call" | custom-call | tf_op jit(solution)/shard_map/inject/pallas_call | solution.py:506
  36.8 23.7 %second_conv_and_exchange.1 = bf16[96,96,128]{2,1,0:T(8,128)(2,1)} custom-call(s32[2,4]{1,0:T(2,128)} %bitcast.11, s32[2,4]{1,0:T(2,128)} %bitcast.13, bf16[9,128,128]{2,1,0:T(8,128)(2,1)} %taps.3, f32[1,128]{1,0:T(1,128)} %bitcast.14, bf16[96,96,128]{2,1,0:T(8,128)(2,1)} %get-tuple-element.14.grid, bf16[24,16,128]{2,1,0:T(8,128)(2,1)} %get-tuple-element.15.pw, ...), custom_call_target="tpu_custom_call" | custom-call | tf_op jit(solution)/shard_map/second_conv_and_exchange/pallas_call | solution.py:522
  60.5 3.2 %copy.13 = bf16[96,96,128]{2,1,0:T(8,128)(2,1)} copy(bf16[96,96,128]{2,1,0:T(8,128)(2,1)} %second_conv_and_exchange.1) | data formatting | bytes 4718592

commit v3 on v2

--- a/solution.py
+++ b/solution.py
@@ -13,6 +13,8 @@
 LANES = 128
 EDGE = 16
 STEP = 8
+GROUP = 8
+REPEAT = 1 << 14
 VMEM_LIMIT = 56 * 1024 * 1024
 
 
@@ -52,7 +54,7 @@
     ).astype(jnp.bfloat16)
 
 
-def pack_observations(dest_count, slots, cell_total, owner_ref, cells_ref, values_ref, rows_out, cells_out):
+def rank_observations(dest_count, slots, owner_ref, cells_ref):
     obs = owner_ref.shape[1]
     owner = owner_ref[...]
     dests = lax.broadcasted_iota(jnp.int32, (dest_count, obs), 0)
@@ -71,22 +73,27 @@
     kind = lax.broadcasted_iota(jnp.int32, (8, obs), 0)
     codes = jnp.where(kind == 0, cells >> 7, jnp.where(kind == 1, cells & 127, 1))
     codes = codes.astype(jnp.float32).astype(jnp.bfloat16)
-    values = values_ref[...]
-    cells_out[...] = jnp.full(cells_out.shape, cell_total, jnp.int32)
-    block = min(512, dest_count * slots)
-    for base in range(0, dest_count * slots, block):
-        wanted = base + lax.broadcasted_iota(jnp.int32, (block, obs), 0)
-        match = jnp.where(wanted == target, 1.0, 0.0).astype(jnp.bfloat16)
-        rows = jnp.dot(match, values, preferred_element_type=jnp.float32).astype(jnp.bfloat16)
-        first = base // slots
-        rows_out[first : first + block // slots] = rows.reshape(block // slots, slots, rows.shape[-1])
-        got = lax.dot_general(
-            codes, match, (((1,), (1,)), ((), ())), preferred_element_type=jnp.float32
-        )
-        found = (got[0:1] * LANES + got[1:2]).astype(jnp.int32)
-        found = jnp.where(got[2:3] > 0.5, found, cell_total)
-        for j in range(block // slots):
-            cells_out[first + j, :, :slots] = found[:, j * slots : (j + 1) * slots]
+    return target, codes
+
+
+def pack_block(block, slots, cell_total, face, target, codes, values, rows_out, cells_out):
+    obs = target.shape[1]
+    first = face * (block // slots)
+    wanted = face * block + lax.broadcasted_iota(jnp.int32, (block, obs), 0)
+    match = jnp.where(wanted == target, 1.0, 0.0).astype(jnp.bfloat16)
+    rows = jnp.dot(match, values[...], preferred_element_type=jnp.float32).astype(jnp.bfloat16)
+    rows_out[pl.ds(first, block // slots)] = rows.reshape(block // slots, slots, rows.shape[-1])
+    got = lax.dot_general(codes, match, (((1,), (1,)), ((), ())), preferred_element_type=jnp.float32)
+    found = (got[0:1] * LANES + got[1:2]).astype(jnp.int32)
+    found = jnp.broadcast_to(jnp.where(got[2:3] > 0.5, found, cell_total), (8, block))
+    place = lax.broadcasted_iota(jnp.int32, (8, block), 1) & (GROUP - 1)
+    repeats = jnp.zeros((8, block), jnp.int32)
+    for k in range(1, GROUP):
+        same = (found == pltpu.roll(found, k, 1)) & (place >= k) & (found < cell_total)
+        repeats = jnp.where(same, REPEAT, repeats)
+    found = found + repeats
+    for j in range(block // slots):
+        cells_out[first + j, :, :slots] = found[:1, j * slots : (j + 1) * slots]
 
 
 def halo_sends(faces, tiles, d, grid, pw, pe, hw, he, north, south, corners, polar):
@@ -256,6 +263,8 @@
     own = own_polar(grid, polar, d, tiles, own_sem.at[2])
     for cond, copy in own:
         guarded(cond, copy.start)
+    cells_out[...] = jnp.full(cells_out.shape, cell_total, jnp.int32)
+    target, codes = rank_observations(count, slots, owner, cells)
     load.wait()
     pw[...] = pack_columns(pad[d : d + rows, :EDGE].astype(jnp.float32), d, False)
     pe[...] = pack_columns(pad[d : d + rows, cols - EDGE : cols].astype(jnp.float32), d, True)
@@ -264,33 +273,43 @@
         halo_sends(faces, tiles, d, grid, pw, pe, hw, he, north, south, corners, polar), send_sem, recv_sem
     )
 
-    pack_observations(count, slots, cell_total, owner, cells, values, rows_out, cells_out)
-
-    def row_copy(k):
-        other, to = device(k)
+    def row_copy(other):
+        to = (other // tiles, lax.rem(other, tiles))
         return pltpu.make_async_remote_copy(
             src_ref=rows_out.at[other], dst_ref=rows_in.at[me],
-            send_sem=row_send.at[k], recv_sem=row_recv.at[k], device_id=to, device_id_type=MESH,
+            send_sem=row_send.at[lax.rem(other + count - me, count)],
+            recv_sem=row_recv.at[lax.rem(other + count - me, count)],
+            device_id=to, device_id_type=MESH,
         )
 
-    def cell_copy(k):
-        other, to = device(k)
+    def cell_copy(other):
+        to = (other // tiles, lax.rem(other, tiles))
         return pltpu.make_async_remote_copy(
             src_ref=cells_out.at[other], dst_ref=cells_in.at[me],
-            send_sem=cell_send.at[k], recv_sem=cell_recv.at[k], device_id=to, device_id_type=MESH,
+            send_sem=cell_send.at[lax.rem(other + count - me, count)],
+            recv_sem=cell_recv.at[lax.rem(other + count - me, count)],
+            device_id=to, device_id_type=MESH,
         )
 
-    def send(k, carry):
-        row_copy(k).start()
-        cell_copy(k).start()
+    def finish(k, carry):
+        other = lax.rem(me + k, count)
+        row_copy(other).wait()
+        cell_copy(other).wait()
         return carry
 
-    def finish(k, carry):
-        row_copy(k).wait()
-        cell_copy(k).wait()
-        return carry
-
-    lax.fori_loop(1, count, send, 0)
+    s, t = lax.axis_index("face"), lax.axis_index("tile")
+    for b in range(1, faces + 1):
+        face = lax.rem(s + b, faces)
+        pack_block(tiles * slots, slots, cell_total, face, target, codes, values, rows_out, cells_out)
+
+        def send(k, carry, face=face):
+            other = face * tiles + lax.rem(t + k, tiles)
+            row_copy(other).start()
+            cell_copy(other).start()
+            return carry
+
+        lax.fori_loop(1 if b == faces else 0, tiles, send, 0)
+
     own_rows = pltpu.make_async_copy(rows_out.at[me], rows_in.at[me], own_sem.at[0])
     own_cells = pltpu.make_async_copy(cells_out.at[me], cells_in.at[me], own_sem.at[1])
     own_rows.start()
@@ -335,17 +354,28 @@
     )
     total[cell_total:] = jnp.zeros((total.shape[0] - cell_total, channels), jnp.float32)
     load.wait()
-    group = 8
+    group = GROUP
 
     def add_group(i, carry):
         source, at = i // (slots // group), lax.rem(i, slots // group) * group
-
-        @pl.when(cells[source, at] < cell_total)
+        marked = [cells[source, at + j] for j in range(group)]
+
+        @pl.when(marked[0] < cell_total)
         def _():
+            any_repeat = functools.reduce(lambda x, y: x | y, marked) & REPEAT
+            places = [m & (REPEAT - 1) for m in marked]
             chunk = encoded[pl.ds(pl.multiple_of(i * group, group), group)]
-            for j in range(group):
-                place = cells[source, at + j]
-                total[pl.ds(place, 1)] += chunk[j : j + 1]
+
+            @pl.when(any_repeat == 0)
+            def _():
+                sums = [total[pl.ds(places[j], 1)] + chunk[j : j + 1] for j in range(group)]
+                for j in range(group):
+                    total[pl.ds(places[j], 1)] = sums[j]
+
+            @pl.when(any_repeat != 0)
+            def _():
+                for j in range(group):
+                    total[pl.ds(places[j], 1)] += chunk[j : j + 1]
 
         return carry
 

time: 63.7 us -> 63.8 us (level); the launches traced: 63.7 us -> 62.8 us
  Pallas kernels: 60.4 us -> 59.6 us
    pallas_call x1, Pallas kernels: 23.7 us -> 21.2 us  [local(): pl.pallas_call(functools.partial(second_kernel, faces, tiles, d2), out_sh...]
    pallas_call x1, Pallas kernels: 12.9 us -> 14.4 us  [local(): pl.pallas_call(functools.partial(inject_kernel, d2), out_shape=[shape((ro...]
where the time goes in v3:
time: 63.8 us; the launch traced here: 62.8 us
  Pallas kernels  59.6 us (93%)
  local copies, waits for them, and re-layouts  3.22 us (5%)
    pallas_call x1, Pallas kernels, local(): pl.pallas_call(functools.partial(first_kernel, faces, tiles, d1, slots),...  24 us
    pallas_call x1, Pallas kernels, local(): pl.pallas_call(functools.partial(second_kernel, faces, tiles, d2), out_sh...  21.2 us
    pallas_call x1, Pallas kernels, local(): pl.pallas_call(functools.partial(inject_kernel, d2), out_shape=[shape((ro...  14.4 us
    unnamed x1, local copies, waits for them, and re-layouts  3.22 us

profile of v3, /device:TPU:0, one launch (start us, length us, event | category | flops | bytes accessed | tf_op | source)
XLA Modules:
  0.0 62.8 jit_solution(1085109715748690803)
XLA Ops:
  0.0 24.0 %first_conv_and_exchange.1 = (f32[9216,128]{1,0:T(8,128)}, bf16[32,64,128]{2,1,0:T(8,128)(2,1)}, s32[32,1,128]{2,1,0:T(1,128)}) custom-call(s32[2,4]{1,0:T(2,128)} %bitcast.10, s32[2,4]{1,0:T(2,128)} %bitcast.12, s32[1,1024]{1,0:T(1,128)} %bitcast.8, s32[1,1024]{1,0:T(1,128)} %bitcast.9, bf16[1024,128]{1,0:T(8,128)(2,1)} %values.1, ...), custom_call_target="tpu_custom_call" | custom-call | tf_op jit(solution)/shard_map/first_conv_and_exchange/pallas_call | solution.py:509
  24.0 14.4 %inject.1 = (bf16[96,96,128]{2,1,0:T(8,128)(2,1)}, bf16[24,16,128]{2,1,0:T(8,128)(2,1)}, bf16[24,16,128]{2,1,0:T(8,128)(2,1)}) custom-call(s32[32,128]{1,0:T(8,128)} %bitcast.7, f32[9216,128]{1,0:T(8,128)} %get-tuple-element.12.first, bf16[32,64,128]{2,1,0:T(8,128)(2,1)} %get-tuple-element.13.values, bf16[128,128]{1,0:T(8,128)(2,1)} %weight.1), custom_call_target="tpu_custom_call" | custom-call | tf_op jit(solution)/shard_map/inject/pallas_call | solution.py:536
  38.4 21.2 %second_conv_and_exchange.1 = bf16[96,96,128]{2,1,0:T(8,128)(2,1)} custom-call(s32[2,4]{1,0:T(2,128)} %bitcast.11, s32[2,4]{1,0:T(2,128)} %bitcast.13, bf16[9,128,128]{2,1,0:T(8,128)(2,1)} %taps.3, f32[1,128]{1,0:T(1,128)} %bitcast.14, bf16[96,96,128]{2,1,0:T(8,128)(2,1)} %get-tuple-element.14.grid, bf16[24,16,128]{2,1,0:T(8,128)(2,1)} %get-tuple-element.15.pw, ...), custom_call_target="tpu_custom_call" | custom-call | tf_op jit(solution)/shard_map/second_conv_and_exchange/pallas_call | solution.py:552
  59.6 3.2 %copy.13 = bf16[96,96,128]{2,1,0:T(8,128)(2,1)} copy(bf16[96,96,128]{2,1,0:T(8,128)(2,1)} %second_conv_and_exchange.1) | data formatting | bytes 4718592

commit v4 on v3

--- a/solution.py
+++ b/solution.py
@@ -13,7 +13,7 @@
 LANES = 128
 EDGE = 16
 STEP = 8
-GROUP = 8
+GROUP = 16
 REPEAT = 1 << 14
 VMEM_LIMIT = 56 * 1024 * 1024
 
@@ -235,6 +235,66 @@
     return [(m * 2 * d + j * d, halves[j][m * d : (m + 1) * d]) for m in range(count) for j in range(2)]
 
 
+def fill_edge_taps(taps, edge_taps):
+    channels, features = taps.shape[1], taps.shape[2]
+    for a in range(3):
+        for i, e in enumerate((0, 2)):
+            edge_taps[a * channels : (a + 1) * channels, i * features : (i + 1) * features] = taps[3 * a + e]
+
+
+def conv_inner(pad, wide_taps, bias, d, start, cols, edges):
+    features = bias.shape[-1]
+    count = STEP // (2 * d)
+    lines = []
+    for k in range(4):
+        blocks = [pad[pl.ds(start + m * 2 * d + k * d, d), :cols] for m in range(count)]
+        lines.append(jnp.concatenate(blocks, axis=0).reshape(count * d * cols, pad.shape[-1]))
+    product = jnp.dot(
+        jnp.concatenate(lines, axis=1), wide_taps[...], preferred_element_type=jnp.float32
+    ).reshape(count * d, cols, 6 * features)
+    shift = bias[...].reshape(1, 1, features)
+    sub = lax.broadcasted_iota(jnp.int32, (count * d, 8, features), 1)
+    pieces = []
+    for j in range(2):
+        low, middle, high = (
+            product[:, :, (2 * e + j) * features : (2 * e + j + 1) * features] for e in range(3)
+        )
+        low = pltpu.roll(low, d, 1)
+        high = pltpu.roll(high, cols - d, 1)
+        middle = middle + shift
+        left = middle[:, :8] + high[:, :8] + jnp.where(sub < d, 0.0, low[:, :8])
+        right = middle[:, cols - 8 :] + low[:, cols - 8 :] + jnp.where(sub >= 8 - d, 0.0, high[:, cols - 8 :])
+        total = low + middle + high
+        for m in range(count):
+            offset = m * 2 * d + j * d
+            edges[0, pl.ds(start + offset, d)] = left[m * d : (m + 1) * d]
+            edges[1, pl.ds(start + offset, d)] = right[m * d : (m + 1) * d]
+            pieces.append((offset, total[m * d : (m + 1) * d]))
+    return pieces
+
+
+def finish_edges(pad, edge_taps, d, start, size, cols, edges, held, out):
+    features = edges.shape[-1]
+    lines = [
+        pad[pl.ds(start + a * d, size), cols:].reshape(size * EDGE, pad.shape[-1]) for a in range(3)
+    ]
+    product = jnp.dot(
+        jnp.concatenate(lines, axis=1), edge_taps[...], preferred_element_type=jnp.float32
+    ).reshape(size, EDGE, 2 * features)
+    sub = lax.broadcasted_iota(jnp.int32, (size, 8, features), 1)
+    here = pl.ds(start, size)
+    from_west = pltpu.roll(product[:, 8:, :features], d, 1)
+    left = edges[0, here] + jnp.where(sub < d, from_west, 0.0)
+    from_east = pltpu.roll(product[:, :8, features:], 8 - d, 1)
+    right = edges[1, here] + jnp.where(sub >= 8 - d, from_east, 0.0)
+    kept = out[here, :EDGE].astype(jnp.float32)[:, 8:]
+    fresh = held[here, :EDGE].astype(jnp.float32)[:, :8] + jax.nn.gelu(left, approximate=True)
+    out[here, :EDGE] = jnp.concatenate([fresh, kept], axis=1).astype(jnp.bfloat16)
+    kept = out[here, cols - EDGE :].astype(jnp.float32)[:, :8]
+    fresh = held[here, cols - EDGE :].astype(jnp.float32)[:, 8:] + jax.nn.gelu(right, approximate=True)
+    out[here, cols - EDGE :] = jnp.concatenate([kept, fresh], axis=1).astype(jnp.bfloat16)
+
+
 def first_kernel(
     faces, tiles, d, slots,
     link, turn, owner, cells, values, taps, bias, grid,
@@ -328,19 +388,25 @@
 
     steps = rows // STEP
     lax.fori_loop(1, steps - 1, step, 0, unroll=2)
+    stores = []
+    for i, (begin, size) in enumerate([(STEP, rows - 2 * STEP), (0, STEP), (rows - STEP, STEP)]):
+        part = pl.ds(begin * cols, size * cols)
+        stores.append(pltpu.make_async_copy(held.at[part], first.at[part], own_sem.at[4 + i]))
+    stores[0].start()
     wait_received(copies[2:])
     for cond, copy in own:
         guarded(cond, copy.wait)
     fill_ends(faces, tiles, d, pad, rows, cols, north, south, corners, polar, link, turn)
     step(0, 0)
     step(steps - 1, 0)
-    store = pltpu.make_async_copy(held, first, own_sem.at[4])
-    store.start()
+    stores[1].start()
+    stores[2].start()
     wait_sent(copies)
     own_rows.wait()
     own_cells.wait()
     lax.fori_loop(1, count, finish, 0)
-    store.wait()
+    for store in stores:
+        store.wait()
 
 
 def inject_kernel(d_next, cells, first, values, weight, mixed, pw_out, pe_out, total, encoded, sem):
@@ -364,18 +430,20 @@
         def _():
             any_repeat = functools.reduce(lambda x, y: x | y, marked) & REPEAT
             places = [m & (REPEAT - 1) for m in marked]
-            chunk = encoded[pl.ds(pl.multiple_of(i * group, group), group)]
+
+            def row(j):
+                return encoded[pl.ds(i * group + j, 1)]
 
             @pl.when(any_repeat == 0)
             def _():
-                sums = [total[pl.ds(places[j], 1)] + chunk[j : j + 1] for j in range(group)]
+                sums = [total[pl.ds(places[j], 1)] + row(j) for j in range(group)]
                 for j in range(group):
                     total[pl.ds(places[j], 1)] = sums[j]
 
             @pl.when(any_repeat != 0)
             def _():
                 for j in range(group):
-                    total[pl.ds(places[j], 1)] += chunk[j : j + 1]
+                    total[pl.ds(places[j], 1)] += row(j)
 
         return carry
 
@@ -395,7 +463,8 @@
 def second_kernel(
     faces, tiles, d, link, turn, taps, bias, grid, pw, pe, fields,
     out,
-    pad, wide_taps, held, hw, he, north, south, corners, polar, send_sem, recv_sem, own_sem,
+    pad, wide_taps, held, edge_taps, edges, hw, he, north, south, corners, polar,
+    send_sem, recv_sem, own_sem,
 ):
     rows, cols, channels = grid.shape
     s, t = lax.axis_index("face"), lax.axis_index("tile")
@@ -445,28 +514,36 @@
         halo_sends(faces, tiles, d, grid, pw, pe, hw, he, north, south, corners, polar), send_sem, recv_sem
     )
     fill_taps(taps, wide_taps)
+    fill_edge_taps(taps, edge_taps)
     load.wait()
     load_fields.wait()
-    wait_received(copies[:2])
-    fill_columns(d, pad, rows, cols, hw, he)
-
-    def step(i, carry):
-        start = i * STEP
-        for offset, piece in conv_rows(pad, wide_taps, bias, d, start, cols):
+
+    def write(start, pieces):
+        for offset, piece in pieces:
             here = held[pl.ds(start + offset, d)].astype(jnp.float32)
             out[pl.ds(start + offset, d)] = (
                 here + jax.nn.gelu(piece, approximate=True)
             ).astype(jnp.bfloat16)
+
+    def inner(i, carry):
+        write(i * STEP, conv_inner(pad, wide_taps, bias, d, i * STEP, cols, edges))
         return carry
 
+    def finish(i, carry):
+        finish_edges(pad, edge_taps, d, i * 2 * STEP + STEP, 2 * STEP, cols, edges, held, out)
+        return carry
+
     steps = rows // STEP
-    lax.fori_loop(1, steps - 1, step, 0, unroll=2)
+    lax.fori_loop(1, steps - 1, inner, 0, unroll=2)
+    wait_received(copies[:2])
+    fill_columns(d, pad, rows, cols, hw, he)
+    lax.fori_loop(0, (steps - 2) // 2, finish, 0)
     wait_received(copies[2:])
     for cond, copy in own:
         guarded(cond, copy.wait)
     fill_ends(faces, tiles, d, pad, rows, cols, north, south, corners, polar, link, turn)
-    step(0, 0)
-    step(steps - 1, 0)
+    for start in (0, rows - STEP):
+        write(start, conv_rows(pad, wide_taps, bias, d, start, cols))
     wait_sent(copies)
 
 
@@ -522,7 +599,7 @@
             pltpu.VMEM(packed_dims(d1), bf16), pltpu.VMEM(packed_dims(d1), bf16),
         ] + halo_scratch(d1) + [
             dma((halo_copies,)), dma((halo_copies,)), dma((dest_count,)), dma((dest_count,)),
-            dma((dest_count,)), dma((dest_count,)), dma((5,)),
+            dma((dest_count,)), dma((dest_count,)), dma((7,)),
         ],
         compiler_params=pltpu.CompilerParams(
             collective_id=0, has_side_effects=True, vmem_limit_bytes=VMEM_LIMIT
@@ -554,8 +631,11 @@
         out_shape=shape((rows, cols, channels), bf16),
         in_specs=[smem] * 2 + [vmem] * 2 + [anywhere] * 4,
         out_specs=vmem,
-        scratch_shapes=conv_scratch(d2) + [pltpu.VMEM((rows, cols, channels), bf16)]
-        + halo_scratch(d2) + [dma((halo_copies,)), dma((halo_copies,)), dma((3,))],
+        scratch_shapes=conv_scratch(d2) + [
+            pltpu.VMEM((rows, cols, channels), bf16),
+            pltpu.VMEM((3 * channels, 2 * channels), bf16),
+            pltpu.VMEM((2, rows, 8, channels), f32),
+        ] + halo_scratch(d2) + [dma((halo_copies,)), dma((halo_copies,)), dma((3,))],
         compiler_params=pltpu.CompilerParams(
             collective_id=1, has_side_effects=True, vmem_limit_bytes=VMEM_LIMIT
         ),

time: 63.8 us -> 61.4 us (0.962); the launches traced: 62.8 us -> 61.1 us
  Pallas kernels: 59.6 us -> 57.8 us
    pallas_call x1, Pallas kernels: 21.2 us -> 18.3 us  [local(): pl.pallas_call(functools.partial(second_kernel, faces, tiles, d2), out_sh...]
    pallas_call x1, Pallas kernels: 14.4 us -> 15.5 us  [local(): pl.pallas_call(functools.partial(inject_kernel, d2), out_shape=[shape((ro...]
where the time goes in v4:
time: 61.4 us; the launch traced here: 61.1 us
  Pallas kernels  57.8 us (94%)
  local copies, waits for them, and re-layouts  3.22 us (5%)
    pallas_call x1, Pallas kernels, local(): pl.pallas_call(functools.partial(first_kernel, faces, tiles, d1, slots),...  24 us
    pallas_call x1, Pallas kernels, local(): pl.pallas_call(functools.partial(second_kernel, faces, tiles, d2), out_sh...  18.3 us
    pallas_call x1, Pallas kernels, local(): pl.pallas_call(functools.partial(inject_kernel, d2), out_shape=[shape((ro...  15.5 us
    unnamed x1, local copies, waits for them, and re-layouts  3.22 us

profile of v4, /device:TPU:0, one launch (start us, length us, event | category | flops | bytes accessed | tf_op | source)
XLA Modules:
  0.0 61.1 jit_solution(16802844716607191496)
XLA Ops:
  0.0 24.0 %first_conv_and_exchange.1 = (f32[9216,128]{1,0:T(8,128)}, bf16[32,64,128]{2,1,0:T(8,128)(2,1)}, s32[32,1,128]{2,1,0:T(1,128)}) custom-call(s32[2,4]{1,0:T(2,128)} %bitcast.10, s32[2,4]{1,0:T(2,128)} %bitcast.12, s32[1,1024]{1,0:T(1,128)} %bitcast.8, s32[1,1024]{1,0:T(1,128)} %bitcast.9, bf16[1024,128]{1,0:T(8,128)(2,1)} %values.1, ...), custom_call_target="tpu_custom_call" | custom-call | tf_op jit(solution)/shard_map/first_conv_and_exchange/pallas_call | solution.py:586
  24.0 15.5 %inject.1 = (bf16[96,96,128]{2,1,0:T(8,128)(2,1)}, bf16[24,16,128]{2,1,0:T(8,128)(2,1)}, bf16[24,16,128]{2,1,0:T(8,128)(2,1)}) custom-call(s32[32,128]{1,0:T(8,128)} %bitcast.7, f32[9216,128]{1,0:T(8,128)} %get-tuple-element.12.first, bf16[32,64,128]{2,1,0:T(8,128)(2,1)} %get-tuple-element.13.values, bf16[128,128]{1,0:T(8,128)(2,1)} %weight.1), custom_call_target="tpu_custom_call" | custom-call | tf_op jit(solution)/shard_map/inject/pallas_call | solution.py:613
  39.5 18.3 %second_conv_and_exchange.1 = bf16[96,96,128]{2,1,0:T(8,128)(2,1)} custom-call(s32[2,4]{1,0:T(2,128)} %bitcast.11, s32[2,4]{1,0:T(2,128)} %bitcast.13, bf16[9,128,128]{2,1,0:T(8,128)(2,1)} %taps.3, f32[1,128]{1,0:T(1,128)} %bitcast.14, bf16[96,96,128]{2,1,0:T(8,128)(2,1)} %get-tuple-element.14.grid, bf16[24,16,128]{2,1,0:T(8,128)(2,1)} %get-tuple-element.15.pw, ...), custom_call_target="tpu_custom_call" | custom-call | tf_op jit(solution)/shard_map/second_conv_and_exchange/pallas_call | solution.py:629
  57.9 3.2 %copy.13 = bf16[96,96,128]{2,1,0:T(8,128)(2,1)} copy(bf16[96,96,128]{2,1,0:T(8,128)(2,1)} %second_conv_and_exchange.1) | data formatting | bytes 4718592

commit v5 on v4

--- a/solution.py
+++ b/solution.py
@@ -15,6 +15,7 @@
 STEP = 8
 GROUP = 16
 REPEAT = 1 << 14
+CHUNKS = 4
 VMEM_LIMIT = 56 * 1024 * 1024
 
 
@@ -409,17 +410,26 @@
         store.wait()
 
 
-def inject_kernel(d_next, cells, first, values, weight, mixed, pw_out, pe_out, total, encoded, sem):
+def inject_kernel(
+    d_next, cells, first, values, weight, mixed_out, pw_out, pe_out,
+    total, encoded, held, mixed, load_sem, store_sem,
+):
     rows, cols, channels = mixed.shape
     sources, slots, features = values.shape
     cell_total = rows * cols
-    load = pltpu.make_async_copy(first, total.at[pl.ds(0, cell_total)], sem)
-    load.start()
+    size = rows // CHUNKS
+    loads, stores = [], []
+    for c in range(CHUNKS):
+        part = pl.ds(c * size * cols, size * cols)
+        loads.append(pltpu.make_async_copy(first.at[part], held.at[part], load_sem.at[c]))
+        part = pl.ds(c * size, size)
+        stores.append(pltpu.make_async_copy(mixed.at[part], mixed_out.at[part], store_sem.at[c]))
+    for load in loads:
+        load.start()
     encoded[...] = jnp.dot(
         values[...].reshape(sources * slots, features), weight[...], preferred_element_type=jnp.float32
     )
-    total[cell_total:] = jnp.zeros((total.shape[0] - cell_total, channels), jnp.float32)
-    load.wait()
+    total[...] = jnp.zeros_like(total)
     group = GROUP
 
     def add_group(i, carry):
@@ -451,19 +461,24 @@
 
     def step(i, carry):
         at = pl.multiple_of(i * STEP * cols, STEP * cols)
-        here = total[pl.ds(at, STEP * cols)].reshape(STEP, cols, channels)
-        mixed[pl.ds(i * STEP, STEP)] = here.astype(jnp.bfloat16)
+        here = held[pl.ds(at, STEP * cols)] + total[pl.ds(at, STEP * cols)]
+        mixed[pl.ds(i * STEP, STEP)] = here.astype(jnp.bfloat16).reshape(STEP, cols, channels)
         return carry
 
-    lax.fori_loop(0, rows // STEP, step, 0)
+    for c in range(CHUNKS):
+        loads[c].wait()
+        lax.fori_loop(c * size // STEP, (c + 1) * size // STEP, step, 0)
+        stores[c].start()
     pw_out[...] = pack_columns(mixed[:, :EDGE].astype(jnp.float32), d_next, False)
     pe_out[...] = pack_columns(mixed[:, cols - EDGE :].astype(jnp.float32), d_next, True)
+    for store in stores:
+        store.wait()
 
 
 def second_kernel(
     faces, tiles, d, link, turn, taps, bias, grid, pw, pe, fields,
-    out,
-    pad, wide_taps, held, edge_taps, edges, hw, he, north, south, corners, polar,
+    out_ref,
+    out, pad, wide_taps, held, edge_taps, edges, hw, he, north, south, corners, polar,
     send_sem, recv_sem, own_sem,
 ):
     rows, cols, channels = grid.shape
@@ -497,10 +512,18 @@
     own = own_polar(grid, polar, d, tiles, own_sem.at[0])
     for cond, copy in own:
         guarded(cond, copy.start)
-    load = pltpu.make_async_copy(grid, pad.at[pl.ds(d, rows), pl.ds(0, cols)], own_sem.at[1])
-    load.start()
-    load_fields = pltpu.make_async_copy(fields, held, own_sem.at[2])
-    load_fields.start()
+    half = rows // 2
+    loads = []
+    for c in range(2):
+        part = pl.ds(c * half, half)
+        place = pad.at[pl.ds(d + c * half, half), pl.ds(0, cols)]
+        loads.append((
+            pltpu.make_async_copy(grid.at[part], place, own_sem.at[1 + c]),
+            pltpu.make_async_copy(fields.at[part], held.at[part], own_sem.at[3 + c]),
+        ))
+    for pair in loads:
+        for load in pair:
+            load.start()
 
     @pl.when(polar_end)
     def _():
@@ -515,8 +538,6 @@
     )
     fill_taps(taps, wide_taps)
     fill_edge_taps(taps, edge_taps)
-    load.wait()
-    load_fields.wait()
 
     def write(start, pieces):
         for offset, piece in pieces:
@@ -534,17 +555,30 @@
         return carry
 
     steps = rows // STEP
-    lax.fori_loop(1, steps - 1, inner, 0, unroll=2)
+    ready = (half - d) // STEP
+    for pair, begin, end in ((loads[0], 1, ready), (loads[1], ready, steps - 1)):
+        for load in pair:
+            load.wait()
+        lax.fori_loop(begin, end, inner, 0, unroll=2)
     wait_received(copies[:2])
     fill_columns(d, pad, rows, cols, hw, he)
     lax.fori_loop(0, (steps - 2) // 2, finish, 0)
+    stores = []
+    for i, (begin, size) in enumerate([(STEP, rows - 2 * STEP), (0, STEP), (rows - STEP, STEP)]):
+        part = pl.ds(begin, size)
+        stores.append(pltpu.make_async_copy(out.at[part], out_ref.at[part], own_sem.at[5 + i]))
+    stores[0].start()
     wait_received(copies[2:])
     for cond, copy in own:
         guarded(cond, copy.wait)
     fill_ends(faces, tiles, d, pad, rows, cols, north, south, corners, polar, link, turn)
     for start in (0, rows - STEP):
         write(start, conv_rows(pad, wide_taps, bias, d, start, cols))
+    stores[1].start()
+    stores[2].start()
     wait_sent(copies)
+    for store in stores:
+        store.wait()
 
 
 def local(
@@ -616,11 +650,13 @@
             shape((rows, cols, channels), bf16), shape(packed_dims(d2), bf16), shape(packed_dims(d2), bf16)
         ],
         in_specs=[smem, anywhere, vmem, vmem],
-        out_specs=[vmem] * 3,
+        out_specs=[anywhere, vmem, vmem],
         scratch_shapes=[
             pltpu.VMEM((cell_total + 8, channels), f32),
             pltpu.VMEM((dest_count * slots, channels), f32),
-            dma,
+            pltpu.VMEM((cell_total, channels), f32),
+            pltpu.VMEM((rows, cols, channels), bf16),
+            dma((CHUNKS,)), dma((CHUNKS,)),
         ],
         compiler_params=pltpu.CompilerParams(vmem_limit_bytes=VMEM_LIMIT),
         name="inject",
@@ -630,12 +666,12 @@
         functools.partial(second_kernel, faces, tiles, d2),
         out_shape=shape((rows, cols, channels), bf16),
         in_specs=[smem] * 2 + [vmem] * 2 + [anywhere] * 4,
-        out_specs=vmem,
-        scratch_shapes=conv_scratch(d2) + [
+        out_specs=anywhere,
+        scratch_shapes=[pltpu.VMEM((rows, cols, channels), bf16)] + conv_scratch(d2) + [
             pltpu.VMEM((rows, cols, channels), bf16),
             pltpu.VMEM((3 * channels, 2 * channels), bf16),
             pltpu.VMEM((2, rows, 8, channels), f32),
-        ] + halo_scratch(d2) + [dma((halo_copies,)), dma((halo_copies,)), dma((3,))],
+        ] + halo_scratch(d2) + [dma((halo_copies,)), dma((halo_copies,)), dma((8,))],
         compiler_params=pltpu.CompilerParams(
             collective_id=1, has_side_effects=True, vmem_limit_bytes=VMEM_LIMIT
         ),

time: 61.4 us -> 59.9 us (0.976)
  Pallas kernels: 57.8 us -> 56.1 us
    pallas_call x1, Pallas kernels: 15.5 us -> 11.6 us  [local(): pl.pallas_call(functools.partial(inject_kernel, d2), out_shape=[shape((ro...]
    pallas_call x1, Pallas kernels: 18.3 us -> 20.5 us  [local(): pl.pallas_call(functools.partial(second_kernel, faces, tiles, d2), out_sh...]
where the time goes in v5:
time: 59.9 us; the launch traced here: 59.4 us
  Pallas kernels  56.1 us (94%)
  local copies, waits for them, and re-layouts  3.22 us (5%)
    pallas_call x1, Pallas kernels, local(): pl.pallas_call(functools.partial(first_kernel, faces, tiles, d1, slots),...  24 us
    pallas_call x1, Pallas kernels, local(): pl.pallas_call(functools.partial(second_kernel, faces, tiles, d2), out_sh...  20.5 us
    pallas_call x1, Pallas kernels, local(): pl.pallas_call(functools.partial(inject_kernel, d2), out_shape=[shape((ro...  11.6 us
    unnamed x1, local copies, waits for them, and re-layouts  3.22 us

profile of v5, /device:TPU:0, one launch (start us, length us, event | category | flops | bytes accessed | tf_op | source)
XLA Modules:
  0.0 59.4 jit_solution(9319194006344795474)
XLA Ops:
  0.0 24.0 %first_conv_and_exchange.1 = (f32[9216,128]{1,0:T(8,128)}, bf16[32,64,128]{2,1,0:T(8,128)(2,1)}, s32[32,1,128]{2,1,0:T(1,128)}) custom-call(s32[2,4]{1,0:T(2,128)} %bitcast.10, s32[2,4]{1,0:T(2,128)} %bitcast.12, s32[1,1024]{1,0:T(1,128)} %bitcast.8, s32[1,1024]{1,0:T(1,128)} %bitcast.9, bf16[1024,128]{1,0:T(8,128)(2,1)} %values.1, ...), custom_call_target="tpu_custom_call" | custom-call | tf_op jit(solution)/shard_map/first_conv_and_exchange/pallas_call | solution.py:620
  24.0 11.6 %inject.1 = (bf16[96,96,128]{2,1,0:T(8,128)(2,1)}, bf16[24,16,128]{2,1,0:T(8,128)(2,1)}, bf16[24,16,128]{2,1,0:T(8,128)(2,1)}) custom-call(s32[32,128]{1,0:T(8,128)} %bitcast.7, f32[9216,128]{1,0:T(8,128)} %get-tuple-element.12.first, bf16[32,64,128]{2,1,0:T(8,128)(2,1)} %get-tuple-element.13.values, bf16[128,128]{1,0:T(8,128)(2,1)} %weight.1), custom_call_target="tpu_custom_call" | custom-call | tf_op jit(solution)/shard_map/inject/pallas_call | solution.py:647
  35.6 20.5 %second_conv_and_exchange.1 = bf16[96,96,128]{2,1,0:T(8,128)(2,1)} custom-call(s32[2,4]{1,0:T(2,128)} %bitcast.11, s32[2,4]{1,0:T(2,128)} %bitcast.13, bf16[9,128,128]{2,1,0:T(8,128)(2,1)} %taps.3, f32[1,128]{1,0:T(1,128)} %bitcast.14, bf16[96,96,128]{2,1,0:T(8,128)(2,1)} %get-tuple-element.14.grid, bf16[24,16,128]{2,1,0:T(8,128)(2,1)} %get-tuple-element.15.pw, ...), custom_call_target="tpu_custom_call" | custom-call | tf_op jit(solution)/shard_map/second_conv_and_exchange/pallas_call | solution.py:665
  56.1 3.2 %copy.13 = bf16[96,96,128]{2,1,0:T(8,128)(2,1)} copy(bf16[96,96,128]{2,1,0:T(8,128)(2,1)} %second_conv_and_exchange.1) | data formatting | bytes 4718592

commit v6 on v5

--- a/solution.py
+++ b/solution.py
@@ -166,7 +166,7 @@
     ).astype(jnp.bfloat16)
 
 
-def fill_ends(faces, tiles, d, pad, rows, cols, north, south, corners, polar, link, turn):
+def fill_ends(faces, tiles, d, pad, rows, cols, north, south, corners, polar, link, turn, which, then):
     s, t = lax.axis_index("face"), lax.axis_index("tile")
     wide = cols + EDGE
 
@@ -184,23 +184,31 @@
             line = jnp.concatenate([polar[p, k], edge], axis=0)
             pad[base + i] = jnp.dot(move, line, preferred_element_type=jnp.float32).astype(jnp.bfloat16)
 
-    @pl.when(t == 0)
-    def _():
-        from_pole(0, 0)
+    if which == "poles":
+
+        @pl.when(t == 0)
+        def _():
+            from_pole(0, 0)
+            then(0)
+
+        @pl.when(t == tiles - 1)
+        def _():
+            from_pole(d + rows, 1)
+            then(rows - STEP)
+
+        return
 
     @pl.when(t > 0)
     def _():
         pad[:d, :cols] = north[...]
         pad[:d, cols:] = join_edge(corners[1], corners[0])
-
-    @pl.when(t == tiles - 1)
-    def _():
-        from_pole(d + rows, 1)
+        then(0)
 
     @pl.when(t < tiles - 1)
     def _():
         pad[d + rows :, :cols] = south[...]
         pad[d + rows :, cols:] = join_edge(corners[3], corners[2])
+        then(rows - STEP)
 
 
 def fill_taps(taps, wide_taps):
@@ -394,12 +402,13 @@
         part = pl.ds(begin * cols, size * cols)
         stores.append(pltpu.make_async_copy(held.at[part], first.at[part], own_sem.at[4 + i]))
     stores[0].start()
-    wait_received(copies[2:])
+    ends = (faces, tiles, d, pad, rows, cols, north, south, corners, polar, link, turn)
+    wait_received(copies[2:8])
+    fill_ends(*ends, "tiles", lambda start: step(start // STEP, 0))
+    wait_received(copies[8:])
     for cond, copy in own:
         guarded(cond, copy.wait)
-    fill_ends(faces, tiles, d, pad, rows, cols, north, south, corners, polar, link, turn)
-    step(0, 0)
-    step(steps - 1, 0)
+    fill_ends(*ends, "poles", lambda start: step(start // STEP, 0))
     stores[1].start()
     stores[2].start()
     wait_sent(copies)
@@ -568,12 +577,17 @@
         part = pl.ds(begin, size)
         stores.append(pltpu.make_async_copy(out.at[part], out_ref.at[part], own_sem.at[5 + i]))
     stores[0].start()
-    wait_received(copies[2:])
+
+    def finish_end(start):
+        write(start, conv_rows(pad, wide_taps, bias, d, start, cols))
+
+    ends = (faces, tiles, d, pad, rows, cols, north, south, corners, polar, link, turn)
+    wait_received(copies[2:8])
+    fill_ends(*ends, "tiles", finish_end)
+    wait_received(copies[8:])
     for cond, copy in own:
         guarded(cond, copy.wait)
-    fill_ends(faces, tiles, d, pad, rows, cols, north, south, corners, polar, link, turn)
-    for start in (0, rows - STEP):
-        write(start, conv_rows(pad, wide_taps, bias, d, start, cols))
+    fill_ends(*ends, "poles", finish_end)
     stores[1].start()
     stores[2].start()
     wait_sent(copies)

time: 59.9 us -> 58.5 us (0.977)
  Pallas kernels: 56.1 us -> 55 us
    pallas_call x1, Pallas kernels: 20.5 us -> 18.3 us  [local(): pl.pallas_call(functools.partial(second_kernel, faces, tiles, d2), out_sh...]
    pallas_call x1, Pallas kernels: 11.6 us -> 12.8 us  [local(): pl.pallas_call(functools.partial(inject_kernel, d2), out_shape=[shape((ro...]
where the time goes in v6:
time: 58.5 us; the launch traced here: 58.3 us
  Pallas kernels  55 us (94%)
  local copies, waits for them, and re-layouts  3.22 us (6%)
    pallas_call x1, Pallas kernels, local(): pl.pallas_call(functools.partial(first_kernel, faces, tiles, d1, slots),...  24 us
    pallas_call x1, Pallas kernels, local(): pl.pallas_call(functools.partial(second_kernel, faces, tiles, d2), out_sh...  18.3 us
    pallas_call x1, Pallas kernels, local(): pl.pallas_call(functools.partial(inject_kernel, d2), out_shape=[shape((ro...  12.8 us
    unnamed x1, local copies, waits for them, and re-layouts  3.22 us

profile of v6, /device:TPU:0, one launch (start us, length us, event | category | flops | bytes accessed | tf_op | source)
XLA Modules:
  0.0 58.3 jit_solution(2092860837642829315)
XLA Ops:
  0.0 24.0 %first_conv_and_exchange.1 = (f32[9216,128]{1,0:T(8,128)}, bf16[32,64,128]{2,1,0:T(8,128)(2,1)}, s32[32,1,128]{2,1,0:T(1,128)}) custom-call(s32[2,4]{1,0:T(2,128)} %bitcast.10, s32[2,4]{1,0:T(2,128)} %bitcast.12, s32[1,1024]{1,0:T(1,128)} %bitcast.8, s32[1,1024]{1,0:T(1,128)} %bitcast.9, bf16[1024,128]{1,0:T(8,128)(2,1)} %values.1, ...), custom_call_target="tpu_custom_call" | custom-call | tf_op jit(solution)/shard_map/first_conv_and_exchange/pallas_call | solution.py:634
  24.0 12.8 %inject.1 = (bf16[96,96,128]{2,1,0:T(8,128)(2,1)}, bf16[24,16,128]{2,1,0:T(8,128)(2,1)}, bf16[24,16,128]{2,1,0:T(8,128)(2,1)}) custom-call(s32[32,128]{1,0:T(8,128)} %bitcast.7, f32[9216,128]{1,0:T(8,128)} %get-tuple-element.12.first, bf16[32,64,128]{2,1,0:T(8,128)(2,1)} %get-tuple-element.13.values, bf16[128,128]{1,0:T(8,128)(2,1)} %weight.1), custom_call_target="tpu_custom_call" | custom-call | tf_op jit(solution)/shard_map/inject/pallas_call | solution.py:661
  36.8 18.3 %second_conv_and_exchange.1 = bf16[96,96,128]{2,1,0:T(8,128)(2,1)} custom-call(s32[2,4]{1,0:T(2,128)} %bitcast.11, s32[2,4]{1,0:T(2,128)} %bitcast.13, bf16[9,128,128]{2,1,0:T(8,128)(2,1)} %taps.3, f32[1,128]{1,0:T(1,128)} %bitcast.14, bf16[96,96,128]{2,1,0:T(8,128)(2,1)} %get-tuple-element.14.grid, bf16[24,16,128]{2,1,0:T(8,128)(2,1)} %get-tuple-element.15.pw, ...), custom_call_target="tpu_custom_call" | custom-call | tf_op jit(solution)/shard_map/second_conv_and_exchange/pallas_call | solution.py:679
  55.1 3.2 %copy.13 = bf16[96,96,128]{2,1,0:T(8,128)(2,1)} copy(bf16[96,96,128]{2,1,0:T(8,128)(2,1)} %second_conv_and_exchange.1) | data formatting | bytes 4718592
